TPU v7x, 32 devices: a whole 2x2x4 slice. The times are simulated.
32 devices in a mesh: tm: 8 (over z, x), space: 4 (over y, core).
Axes of the slice: x: 2, y: 2, z: 4, core: 2. Of those that a mesh axis runs over, the one named last changes fastest.
Arguments:
- increment: float32 [32, 4, 32, 512], P('tm', None, 'space'), may hold values from -6 to 6
- trajectory: float32 [32, 4, 32, 512], P('tm', None, 'space'), may hold values from -6 to 6
- input_weight: float32 [32, 4, 3, 3], replicated, may hold values from -1 to 1
- bias: float32 [32], replicated, may hold values from -4 to 4
- output_weight: float32 [4, 32, 3, 3], replicated, may hold values from -0.375 to 0.375
- correlation: float32 [4, 32, 32], replicated, may hold values from -1 to 4, as said below
Outputs:
- corrected: float32 [32, 4, 32, 512], P('tm', None, 'space')
Inputs may be any that keep to these rules, and one draw needn't show every extreme that they name: `correlation`: each field's matrix is symmetric positive definite.
All inputs are finite; a program needn't handle non-finite values.
Results may differ from a plain program's by a relative error of at most 0.0001.
Values sent between devices are 32-bit elements; how exact they have to be, the bound alone decides.
No kernel may reach another device: no remote copies, remote signals or barrier semaphores. Data moves between devices by JAX's collectives and lax.ppermute only.
A program may use at most 64 MiB of HBM per device.

v0:
```python
import functools

import jax
import jax.numpy as jnp
from jax import lax
from jax.experimental import pallas as pl
from jax.experimental.pallas import tpu as pltpu
from jax.sharding import PartitionSpec as P

STEPS = 2
TENDENCY = 0.5
HALO = 2 * STEPS
F32 = jnp.float32
BF16 = jnp.bfloat16
EXACT = lax.Precision.HIGHEST
VMEM = pl.BlockSpec(memory_space=pltpu.VMEM)

WIN_OUT = 4
LANES = 128
KEYS = 256


def iota(shape, dim):
    return lax.broadcasted_iota(jnp.int32, shape, dim)


def split(value):
    high = value.astype(BF16)
    return high, (value - high.astype(F32)).astype(BF16)


def pack_kernel(traj_ref, incr_ref, head_ref, tail_ref):
    slots, fields, rows, _ = traj_ref.shape
    half = rows // 2
    for kind, ref in enumerate((traj_ref, incr_ref)):
        for slot in range(slots):
            for f in range(fields):
                place = pl.ds(f, half, stride=fields)
                for piece in range(head_ref.shape[1]):
                    columns = slice(piece * LANES, (piece + 1) * LANES)
                    head_ref[kind * slots + slot, piece, place, :] = ref[slot, f, 0:half, columns]
                    tail_ref[kind * slots + slot, piece, place, :] = ref[slot, f, half:rows, columns]


def key_codes(shape, dim):
    key = iota(shape, dim)
    tap = (key >= 48).astype(jnp.int32) + (key >= 96).astype(jnp.int32)
    q = key - 48 * tap
    sub = jnp.where(q < 16, q, jnp.where(q < 32, q - 16, jnp.where(q < 40, q - 16, q - 24)))
    high = jnp.where(key < 144, tap * 24 + sub, -1000)
    rest = key - 144
    tap2 = rest // 32
    q2 = rest - 32 * tap2
    sub2 = jnp.where(q2 < 24, q2, q2 - 8)
    low = jnp.where((key >= 144) & (key < 240), tap2 * 24 + sub2, -1000)
    return high, low, key


def prepare_kernel(edge_ref, w1_ref, bias_ref, w2_ref, corr_ref, w1_out, w2_out, w2_last, mix_out, *, tm, slots):
    channels = w1_ref.shape[0]
    fields = corr_ref.shape[0]
    time = corr_ref.shape[1]
    j = iota((36, KEYS), 0)
    f = (j >= 9).astype(jnp.int32) + (j >= 18).astype(jnp.int32) + (j >= 27).astype(jnp.int32)
    r = j - 9 * f
    a = (r >= 3).astype(jnp.int32) + (r >= 6).astype(jnp.int32)
    b = r - 3 * a
    code = b * 24 + a * 4 + f
    high_code, low_code, _ = key_codes((36, KEYS), 1)
    w_high, w_low = split(w1_ref[...])
    bias = bias_ref[...]
    b0 = bias.astype(BF16).astype(F32)
    b1 = (bias - b0).astype(BF16).astype(F32)
    b2 = bias - b0 - b1
    key = iota((channels, KEYS), 1)
    bias_part = (
        jnp.where(key == 240, b0, 0.0) + jnp.where(key == 241, b1, 0.0) + jnp.where(key == 242, b2, 0.0)
    )
    for out in range(WIN_OUT):
        pick_high = jnp.where(code + 4 * out == high_code, 1.0, 0.0).astype(BF16)
        pick_low = jnp.where(code + 4 * out == low_code, 1.0, 0.0).astype(BF16)
        block = jnp.dot(w_high, pick_high, preferred_element_type=F32)
        block += jnp.dot(w_low, pick_low, preferred_element_type=F32)
        w1_out[out * channels : (out + 1) * channels, :] = (block + bias_part).astype(BF16)
    spread = jnp.where(iota((channels, 8 * channels), 1) % channels == iota((channels, 8 * channels), 0), 1.0, 0.0)
    halves = split(w2_ref[...] * TENDENCY)
    tables = [jnp.dot(h, spread.astype(BF16), preferred_element_type=F32).astype(BF16) for h in halves]
    m = iota((72, 8 * channels), 0)
    m_tap = (m >= 24).astype(jnp.int32) + (m >= 48).astype(jnp.int32)
    m_row = (m - 24 * m_tap) // 4
    k_row = iota((72, 8 * channels), 1) // channels
    mj = iota((72, 36), 0)
    mj_tap = (mj >= 24).astype(jnp.int32) + (mj >= 48).astype(jnp.int32)
    mj_field = mj % 4
    full = []
    for table in tables:
        total = jnp.zeros((72, 8 * channels), F32)
        for tap_row in range(3):
            pick = jnp.where(iota((72, 36), 1) == tap_row * 12 + mj_tap * 4 + mj_field, 1.0, 0.0).astype(BF16)
            part = jnp.dot(pick, table, preferred_element_type=F32)
            total = total + jnp.where(k_row == m_row + tap_row, part, 0.0)
        full.append(total)
    top = edge_ref[0]
    bottom = edge_ref[1]
    keep_top = 1.0 - top.astype(F32)
    keep_bottom = 1.0 - bottom.astype(F32)
    for part, total in enumerate(full):
        w2_out[0, part * 72 : (part + 1) * 72, :] = jnp.where(k_row < 3, total * keep_top, total).astype(BF16)
        w2_out[1, part * 72 : (part + 1) * 72, :] = jnp.where(k_row > 4, total * keep_bottom, total).astype(BF16)
        w2_out[2, part * 72 : (part + 1) * 72, :] = jnp.where(k_row < 1, total * keep_top, total).astype(BF16)
        last = jnp.concatenate([total[0:8], total[24:32], total[48:56]], axis=0)
        last_row = iota((24, 8 * channels), 1) // channels
        last = jnp.where(last_row > 2, last * keep_bottom, last)
        w2_last[part * 24 : (part + 1) * 24, :] = last[:, 0 : 4 * channels].astype(BF16)
    keys = mix_out.shape[1]
    block = (slots + 2) * fields
    key = iota((time, keys), 1)
    sender = key // block
    row = key - sender * block
    slot = slots * sender + row // fields
    valid = row < (slots + 1) * fields
    pick = jnp.where((iota((time, keys), 0) == slot) & valid, 1.0, 0.0)
    total = jnp.zeros(mix_out.shape, F32)
    wide = (time * fields, time)
    repeat = jnp.where(iota(wide, 0) // fields == iota(wide, 1), 1.0, 0.0)
    to_field = iota(mix_out.shape, 0) % fields
    from_field = iota(mix_out.shape, 1) % fields
    for f in range(fields):
        part = jnp.dot(corr_ref[f], pick, precision=EXACT, preferred_element_type=F32)
        part = jnp.dot(repeat, part, precision=EXACT, preferred_element_type=F32)
        total = jnp.where((to_field == f) & (from_field == f), part, total)
    mix_out[...] = total


def moved(value, shift):
    if shift == 0:
        return value
    cols = value.shape[1]
    column = iota(value.shape, 1)
    turned = pltpu.roll(value, shift % cols, 1)
    outside = column == (0 if shift > 0 else cols - 1)
    return jnp.where(outside, 0.0, turned)


def hidden_inputs(groups):
    parts = []
    for tap in range(3):
        highs, lows = [], []
        for group in groups:
            value = moved(group, 1 - tap)
            high = value.astype(BF16).astype(F32)
            highs.append(high)
            lows.append(value - high)
        parts.append((highs, lows))
    return parts


def window(parts, start, ones):
    def tile(first, second):
        return jnp.concatenate([first, second], axis=0).astype(BF16)

    front, back = [], []
    for highs, lows in parts:
        a = tile(highs[start], highs[start + 1])
        b = tile(lows[start], lows[start + 1])
        c = tile(highs[start + 2], lows[start + 2])
        front += [a, b, c]
        back += [a, c]
    return jnp.concatenate(front + back + [ones], axis=0)


def hidden_pair(state_groups, tangent_groups, starts, w1):
    cols = state_groups[0].shape[1]
    one = jnp.ones((16, cols), BF16)
    zero = jnp.zeros((16, cols), BF16)
    state_parts = hidden_inputs(state_groups)
    tangent_parts = hidden_inputs(tangent_groups)
    result = []
    for index, start in enumerate(starts):
        rows = w1 if index < len(starts) - 1 else w1[: w1.shape[0] // 2]
        z = jnp.dot(rows, window(state_parts, start, one), preferred_element_type=F32)
        dz = jnp.dot(rows, window(tangent_parts, start, zero), preferred_element_type=F32)
        h = jnp.tanh(z)
        g = (1.0 - h * h) * dz
        result.append((h, g))
    return result


def output_sum(pieces, weight):
    half = weight.shape[0] // 2
    high = jnp.concatenate([p[0] for p in pieces], axis=0)
    low = jnp.concatenate([p[1] for p in pieces], axis=0)
    both = jnp.dot(weight, high, preferred_element_type=F32)
    taps = both[:half] + both[half:] + jnp.dot(weight[:half], low, preferred_element_type=F32)
    third = half // 3
    return moved(taps[0:third], 1) + taps[third : 2 * third] + moved(taps[2 * third :], -1)


def forecast_kernel(
    edge_ref, head_ref, tail_ref, top_ref, bottom_ref, w1_ref, w2_ref, w2_last_ref, send_ref, done_ref, *, slots, parts_across
):
    channels = w1_ref.shape[0] // WIN_OUT
    pieces = head_ref.shape[1]
    cols = pieces * LANES
    keep_top = 1.0 - edge_ref[0].astype(F32)
    keep_bottom = 1.0 - edge_ref[1].astype(F32)
    blank = jnp.zeros((8, cols), F32)

    def group_of(ref, index, half):
        return jnp.concatenate([ref[index, p, 8 * half : 8 * half + 8, :] for p in range(pieces)], axis=1)

    def one_slot(slot, carry):
        frames = []
        for kind in range(2):
            index = kind * slots + slot
            groups = []
            for ref in (top_ref, head_ref, tail_ref, bottom_ref):
                groups += [group_of(ref, index, 0), group_of(ref, index, 1)]
            frames.append(groups + [blank])
        w1 = w1_ref[...]
        windows = hidden_pair(frames[0], frames[1], (0, 2, 4, 6), w1)
        advanced = []
        for kind in range(2):
            halves = [split(pair[kind]) for pair in windows]
            mid = 2 * channels
            upper = output_sum([halves[0], halves[1]], w2_ref[0])
            lower = output_sum(
                [tuple(p[mid:] for p in halves[1]), halves[2], halves[3]], w2_ref[1]
            )
            groups = [blank] + [frames[kind][g] for g in range(1, 7)] + [blank, blank]
            for g in range(3):
                groups[1 + g] = groups[1 + g] + upper[8 * g : 8 * g + 8]
                groups[4 + g] = groups[4 + g] + lower[8 * g : 8 * g + 8]
            groups[1] = groups[1] * keep_top
            groups[6] = groups[6] * keep_bottom
            advanced.append(groups)
        windows = hidden_pair(advanced[0], advanced[1], (1, 3, 5), w1)
        halves = [split(pair[1]) for pair in windows]
        upper = output_sum([halves[0], halves[1]], w2_ref[2])
        lower = output_sum([tuple(p[2 * channels :] for p in halves[1]), halves[2]], w2_last_ref[...])
        tangent = advanced[1]
        for g in range(3):
            done_ref[slot, 8 * g : 8 * g + 8, :] = tangent[2 + g] + upper[8 * g : 8 * g + 8]
        done_ref[slot, 24:32, :] = tangent[5] + lower
        return carry

    lax.fori_loop(0, slots, one_slot, 0)

    width = cols // parts_across
    fields = 4
    rows = 8
    for slot in range(slots + 1):
        if slot < slots:
            index = slots + slot
            start = jnp.concatenate([group_of(ref, index, h) for ref in (head_ref, tail_ref) for h in range(2)], axis=0)
            value = start - done_ref[slot - 1] if slot else start
        else:
            value = -done_ref[slot - 1]
        for y in range(rows):
            for block in range(parts_across):
                send_ref[y * parts_across + block, slot * fields : (slot + 1) * fields, :] = value[
                    y * fields : (y + 1) * fields, block * width : (block + 1) * width
                ]
    send_ref[:, (slots + 1) * fields :, :] = jnp.zeros((rows * parts_across, fields, width), F32)


def mix_kernel(mix_ref, block_ref, out_ref):
    count, rows, width = block_ref.shape
    keys = block_ref[...].reshape(count * rows, width)
    out = jnp.dot(mix_ref[...], keys, precision=EXACT, preferred_element_type=F32)
    out_ref[...] = out.reshape(out_ref.shape)


def params():
    return pltpu.CompilerParams(vmem_limit_bytes=24 * 1024 * 1024)


def body(increment, trajectory, input_weight, bias, output_weight, correlation):
    slots, fields, rows, cols = increment.shape
    channels = input_weight.shape[0]
    tm = lax.axis_size("tm")
    strips = lax.axis_size("space")
    time = correlation.shape[1]
    parts_across = tm // rows
    width = cols // parts_across
    me = lax.axis_index("space")
    edges = jnp.stack([me == 0, me == strips - 1]).astype(jnp.int32)

    half = jax.ShapeDtypeStruct((2 * slots, cols // LANES, rows // 2 * fields, LANES), F32)
    head, tail = pl.pallas_call(
        pack_kernel, out_shape=(half, half), in_specs=[VMEM] * 2, out_specs=(VMEM, VMEM), compiler_params=params(), name="pack"
    )(trajectory, increment)
    top = lax.ppermute(tail, "space", [(i, i + 1) for i in range(strips - 1)])
    bottom = lax.ppermute(head, "space", [(i + 1, i) for i in range(strips - 1)])

    block_rows = (slots + 2) * fields
    smem = pl.BlockSpec(memory_space=pltpu.SMEM)
    w1, w2, w2_last, mix = pl.pallas_call(
        functools.partial(prepare_kernel, tm=tm, slots=slots),
        out_shape=(
            jax.ShapeDtypeStruct((WIN_OUT * channels, KEYS), BF16),
            jax.ShapeDtypeStruct((3, 144, 8 * channels), BF16),
            jax.ShapeDtypeStruct((48, 4 * channels), BF16),
            jax.ShapeDtypeStruct((time * fields, tm * block_rows), F32),
        ),
        in_specs=[smem] + [VMEM] * 4,
        out_specs=(VMEM,) * 4,
        compiler_params=params(),
        name="prepare",
    )(
        edges,
        input_weight.reshape(channels, -1),
        bias[:, None],
        jnp.transpose(output_weight, (2, 3, 0, 1)).reshape(-1, channels),
        correlation,
    )

    send = pl.pallas_call(
        functools.partial(forecast_kernel, slots=slots, parts_across=parts_across),
        out_shape=jax.ShapeDtypeStruct((tm, block_rows, width), F32),
        in_specs=[smem] + [VMEM] * 7,
        out_specs=VMEM,
        scratch_shapes=[pltpu.VMEM((slots, rows * fields, cols), F32)],
        compiler_params=params(),
        name="forecast",
    )(edges, head, tail, top, bottom, w1, w2, w2_last)

    blocks = lax.all_to_all(send, "tm", split_axis=0, concat_axis=0, tiled=True)
    mixed = pl.pallas_call(
        mix_kernel,
        out_shape=jax.ShapeDtypeStruct((tm, slots * fields, width), F32),
        in_specs=[VMEM] * 2,
        out_specs=VMEM,
        compiler_params=params(),
        name="mix",
    )(mix, blocks)
    back = lax.all_to_all(mixed, "tm", split_axis=0, concat_axis=0, tiled=True)
    back = back.reshape(rows, parts_across, slots, fields, width)
    return jnp.transpose(back, (2, 3, 0, 1, 4)).reshape(slots, fields, rows, cols)


def solution(mesh):
    placed = (P("tm", None, "space", None), P("tm", None, "space", None), P(), P(), P(), P())
    return jax.shard_map(
        body, mesh=mesh, in_specs=placed, out_specs=P("tm", None, "space", None), check_vma=False
    )
```

profile of v0, /device:TPU:0, one launch (start us, length us, event | category | flops | bytes accessed | tf_op | source)
XLA Modules:
  0.0 51.6 jit_solution(8819433113904536499)
XLA Ops:
  0.0 0.0 copy-start
  0.0 0.9 %copy-done = f32[4,4,8,512]{3,2,1,0:T(8,128)S(1)} copy-done((f32[4,4,8,512]{3,2,1,0:T(8,128)S(1)}, f32[4,4,8,512]{3,2,1,0:T(8,128)}, u32[]{:S(2)}) %copy-start) | copy-done | bytes 262168
  1.0 0.0 copy-start.1
  1.0 0.9 %copy-done.1 = f32[4,4,8,512]{3,2,1,0:T(8,128)S(1)} copy-done((f32[4,4,8,512]{3,2,1,0:T(8,128)S(1)}, f32[4,4,8,512]{3,2,1,0:T(8,128)}, u32[]{:S(2)}) %copy-start.1) | copy-done | bytes 262168
  1.9 0.0 copy-start.5
  1.9 0.1 pack.1
  2.0 0.0 copy-start.3
  2.1 1.3 %collective-permute-start.1 = (f32[8,4,16,128]{3,2,1,0:T(8,128)S(1)}, f32[8,4,16,128]{3,2,1,0:T(8,128)S(1)}, u32[]{:S(2)}, u32[]{:S(2)}) collective-permute-start(f32[8,4,16,128]{3,2,1,0:T(8,128)S(1)} %get-tuple-element.12.head_ref), channel_id=1, source_target_pairs={{1,0},{2,1},{3,2},{5,4},{6,5},{7,6},{9,8},{10,9},{11,10},{13,12},{... | collective-permute-start | bytes 786440 | tf_op jit(solution)/shard_map/ppermute | solution.py:294
  3.4 3.0 %collective-permute-start = (f32[8,4,16,128]{3,2,1,0:T(8,128)S(1)}, f32[8,4,16,128]{3,2,1,0:T(8,128)S(1)}, u32[]{:S(2)}, u32[]{:S(2)}) collective-permute-start(f32[8,4,16,128]{3,2,1,0:T(8,128)S(1)} %get-tuple-element.13.tail_ref), channel_id=1, source_target_pairs={{0,1},{1,2},{2,3},{4,5},{5,6},{6,7},{8,9},{9,10},{10,11},{12,13},{... | collective-permute-start | bytes 786440 | tf_op jit(solution)/shard_map/ppermute | solution.py:293
  6.4 0.0 copy-done.5
  6.4 0.1 copy.12.bias_ref
  6.5 0.0 copy-done.3
  6.5 0.0 copy-start.4
  6.5 0.7 %copy-done.4 = f32[32,4,3,3]{0,1,3,2:T(4,128)S(1)} copy-done((f32[32,4,3,3]{0,1,3,2:T(4,128)S(1)}, f32[32,4,3,3]{0,1,3,2:T(4,128)}, u32[]{:S(2)}) %copy-start.4) | copy-done | bytes 4632
  7.2 0.0 copy-start.2
  7.3 0.1 copy.11.w1_ref
  7.4 0.1 add_convert_fusion.edge_ref
  7.4 0.7 %copy-done.2 = f32[4,32,32]{2,1,0:T(8,128)S(1)} copy-done((f32[4,32,32]{2,1,0:T(8,128)S(1)}, f32[4,32,32]{2,1,0:T(8,128)}, u32[]{:S(2)}) %copy-start.2) | copy-done | bytes 16408
  8.1 1.7 %prepare.1 = (bf16[128,256]{1,0:T(8,128)(2,1)S(1)}, bf16[3,144,256]{2,1,0:T(8,128)(2,1)S(1)}, bf16[48,128]{1,0:T(8,128)(2,1)S(1)}, f32[128,192]{1,0:T(8,128)S(1)}) custom-call(s32[2]{0:T(128)S(1)} %add_convert_fusion.edge_ref, f32[32,36]{1,0:T(8,128)S(1)} %copy.11.w1_ref, f32[32,1]{1,0:T(8,128)S(1)} %copy.12.bias_ref, f32[36,32]{1,0:T(8,128)S(1)} %reshape.13.w2_ref, ...), custom_call_target="tpu_custom_call" | custom-call | tf_op jit(solution)/shard_map/prepare/pallas_call | solution.py:298
  9.8 0.0 collective-permute-done.1.bottom_ref
  9.8 0.0 collective-permute-done.top_ref
  9.8 7.9 %forecast.1 = f32[8,24,512]{2,1,0:T(8,128)S(1)} custom-call(s32[2]{0:T(128)S(1)} %add_convert_fusion.edge_ref, f32[8,4,16,128]{3,2,1,0:T(8,128)S(1)} %get-tuple-element.12.head_ref, f32[8,4,16,128]{3,2,1,0:T(8,128)S(1)} %get-tuple-element.13.tail_ref, f32[8,4,16,128]{3,2,1,0:T(8,128)S(1)} %collective-permute-done.top_ref, ...), custom_call_target="tpu_custom_call" | custom-call | tf_op jit(solution)/shard_map/forecast/pallas_call | solution.py:318
  17.7 20.0 %all_to_all.10.block_ref = f32[8,24,512]{2,1,0:T(8,128)S(1)} all-to-all(f32[8,24,512]{2,1,0:T(8,128)S(1)} %forecast.1), channel_id=1, replica_groups=mesh['tm'=8,'space'=4] {'tm'}, dimensions={0} | all-to-all | bytes 786432 | tf_op jit(solution)/shard_map/all_to_all | solution.py:328
  37.7 0.4 mix.1
  38.1 12.6 %all_to_all.11 = f32[8,16,512]{2,1,0:T(8,128)S(1)} all-to-all(f32[8,16,512]{2,1,0:T(8,128)S(1)} %mix.1), channel_id=1, replica_groups=mesh['tm'=8,'space'=4] {'tm'}, dimensions={0} | all-to-all | bytes 524288 | tf_op jit(solution)/shard_map/all_to_all | solution.py:337
  50.7 0.9 %copy.14 = f32[8,16,512]{2,0,1:T(8,128)} copy(f32[8,16,512]{2,1,0:T(8,128)S(1)} %all_to_all.11) | data formatting | bytes 524288 | tf_op jit(solution)/shard_map/reshape | solution.py:338
  (3 shorter events, 0.0 us)
Async XLA Ops:
  0.0 0.9 %copy-start = (f32[4,4,8,512]{3,2,1,0:T(8,128)S(1)}, f32[4,4,8,512]{3,2,1,0:T(8,128)}, u32[]{:S(2)}) copy-start(f32[4,4,8,512]{3,2,1,0:T(8,128)} %traj_ref.1) | copy-start | bytes 786436
  1.0 0.9 %copy-start.1 = (f32[4,4,8,512]{3,2,1,0:T(8,128)S(1)}, f32[4,4,8,512]{3,2,1,0:T(8,128)}, u32[]{:S(2)}) copy-start(f32[4,4,8,512]{3,2,1,0:T(8,128)} %incr_ref.1) | copy-start | bytes 786436
  1.9 4.5 %copy-start.5 = (f32[32]{0:T(128)S(1)}, f32[32]{0:T(128)}, u32[]{:S(2)}) copy-start(f32[32]{0:T(128)} %param.9) | copy-start | bytes 388
  2.0 4.5 %copy-start.3 = (f32[4,32,3,3]{1,0,3,2:T(4,128)S(1)}, f32[4,32,3,3]{1,0,3,2:T(4,128)}, u32[]{:S(2)}) copy-start(f32[4,32,3,3]{1,0,3,2:T(4,128)} %param.10) | copy-start | bytes 13828
  2.1 7.7 %collective-permute-start.1 = (f32[8,4,16,128]{3,2,1,0:T(8,128)S(1)}, f32[8,4,16,128]{3,2,1,0:T(8,128)S(1)}, u32[]{:S(2)}, u32[]{:S(2)}) collective-permute-start(f32[8,4,16,128]{3,2,1,0:T(8,128)S(1)} %get-tuple-element.12.head_ref), channel_id=1, source_target_pairs={{1,0},{2,1},{3,2},{5,4},{6,5},{7,6},{9,8},{10,9},{11,10},{13,12},{... | collective-permute-start | bytes 786440 | tf_op jit(solution)/shard_map/ppermute | solution.py:294
  3.4 6.5 %collective-permute-start = (f32[8,4,16,128]{3,2,1,0:T(8,128)S(1)}, f32[8,4,16,128]{3,2,1,0:T(8,128)S(1)}, u32[]{:S(2)}, u32[]{:S(2)}) collective-permute-start(f32[8,4,16,128]{3,2,1,0:T(8,128)S(1)} %get-tuple-element.13.tail_ref), channel_id=1, source_target_pairs={{0,1},{1,2},{2,3},{4,5},{5,6},{6,7},{8,9},{9,10},{10,11},{12,13},{... | collective-permute-start | bytes 786440 | tf_op jit(solution)/shard_map/ppermute | solution.py:293
  6.5 0.7 %copy-start.4 = (f32[32,4,3,3]{0,1,3,2:T(4,128)S(1)}, f32[32,4,3,3]{0,1,3,2:T(4,128)}, u32[]{:S(2)}) copy-start(f32[32,4,3,3]{0,1,3,2:T(4,128)} %param.8) | copy-start | bytes 13828
  7.2 0.8 %copy-start.2 = (f32[4,32,32]{2,1,0:T(8,128)S(1)}, f32[4,32,32]{2,1,0:T(8,128)}, u32[]{:S(2)}) copy-start(f32[4,32,32]{2,1,0:T(8,128)} %corr_ref.1) | copy-start | bytes 49156
where the time goes:
time: 52 us; the launch traced here: 51.6 us
  blocking collectives  32.6 us (63%)
  Pallas kernels  10.1 us (19%)
  starting transfers between devices  4.34 us (8%)
  local copies, waits for them, and re-layouts  4.33 us (8%)
    all_to_all x1, blocking collectives, body(): blocks = lax.all_to_all(send, 'tm', split_axis=0, concat_axis=0, tiled=True)  20 us
    all_to_all x1, blocking collectives, body(): back = lax.all_to_all(mixed, 'tm', split_axis=0, concat_axis=0, tiled=True)  12.6 us
    pallas_call x1, Pallas kernels, body(): pl.pallas_call(functools.partial(forecast_kernel, slots=slots, parts_acro...  7.87 us
    unnamed x13, local copies, waits for them, and re-layouts  3.28 us
    ppermute x1, starting transfers between devices, body(): top = lax.ppermute(tail, 'space', [(i, i + 1) for i in range(strips - 1)])  3.05 us
    pallas_call x1, Pallas kernels, body(): pl.pallas_call(functools.partial(prepare_kernel, tm=tm, slots=slots), out...  1.7 us
    ppermute x1, starting transfers between devices, body(): lax.ppermute(head, 'space', [(i + 1, i) for i in range(strips - 1)])  1.29 us
  transfers between devices with their start and end apart: 2, of which 0 were waited for; matrix products, arithmetic and copies ran while one was open for 1% of the time, Pallas kernels for 3%

commit v1 on v0

--- a/solution.py
+++ b/solution.py
@@ -29,17 +29,35 @@
     return high, (value - high.astype(F32)).astype(BF16)
 
 
-def pack_kernel(traj_ref, incr_ref, head_ref, tail_ref):
+def pack_kernel(
+    traj_hbm, incr_hbm, w1_hbm, bias_hbm, w2_hbm, corr_hbm,
+    own_ref, core_ref, chip_ref, w1_ref, bias_ref, w2_ref, corr_ref,
+    traj_ref, incr_ref, sems,
+):
+    pairs = (
+        (traj_hbm, traj_ref), (incr_hbm, incr_ref), (w1_hbm, w1_ref), (bias_hbm, bias_ref), (w2_hbm, w2_ref), (corr_hbm, corr_ref)
+    )
+    copies = [pltpu.make_async_copy(src, dst, sems.at[n]) for n, (src, dst) in enumerate(pairs)]
+    for copy in copies:
+        copy.start()
     slots, fields, rows, _ = traj_ref.shape
-    half = rows // 2
+    half = rows // 2 * fields
+    odd = lax.axis_index("space") % 2
+    core_half = pl.ds(pl.multiple_of((1 - odd) * half, half), half)
+    chip_half = pl.ds(pl.multiple_of(odd * half, half), half)
     for kind, ref in enumerate((traj_ref, incr_ref)):
+        copies[kind].wait()
         for slot in range(slots):
-            for f in range(fields):
-                place = pl.ds(f, half, stride=fields)
-                for piece in range(head_ref.shape[1]):
-                    columns = slice(piece * LANES, (piece + 1) * LANES)
-                    head_ref[kind * slots + slot, piece, place, :] = ref[slot, f, 0:half, columns]
-                    tail_ref[kind * slots + slot, piece, place, :] = ref[slot, f, half:rows, columns]
+            index = kind * slots + slot
+            for piece in range(own_ref.shape[1]):
+                for f in range(fields):
+                    own_ref[index, piece, pl.ds(f, rows, stride=fields), :] = ref[
+                        slot, f, :, piece * LANES : (piece + 1) * LANES
+                    ]
+                core_ref[index, piece] = own_ref[index, piece, core_half, :]
+                chip_ref[index, piece] = own_ref[index, piece, chip_half, :]
+    for copy in copies[2:]:
+        copy.wait()
 
 
 def key_codes(shape, dim):
@@ -56,34 +74,30 @@
     return high, low, key
 
 
-def prepare_kernel(edge_ref, w1_ref, bias_ref, w2_ref, corr_ref, w1_out, w2_out, w2_last, mix_out, *, tm, slots):
-    channels = w1_ref.shape[0]
-    fields = corr_ref.shape[0]
+def prepare_kernel(w1_ref, bias_ref, w2_ref, corr_ref, w1_out, w2_out, w2_last, mix_out, *, strips, slots):
+    fields = w1_ref.shape[2]
+    channels = w1_ref.shape[3]
     time = corr_ref.shape[1]
-    j = iota((36, KEYS), 0)
-    f = (j >= 9).astype(jnp.int32) + (j >= 18).astype(jnp.int32) + (j >= 27).astype(jnp.int32)
-    r = j - 9 * f
-    a = (r >= 3).astype(jnp.int32) + (r >= 6).astype(jnp.int32)
-    b = r - 3 * a
-    code = b * 24 + a * 4 + f
-    high_code, low_code, _ = key_codes((36, KEYS), 1)
-    w_high, w_low = split(w1_ref[...])
-    bias = bias_ref[...]
-    b0 = bias.astype(BF16).astype(F32)
-    b1 = (bias - b0).astype(BF16).astype(F32)
-    b2 = bias - b0 - b1
-    key = iota((channels, KEYS), 1)
-    bias_part = (
-        jnp.where(key == 240, b0, 0.0) + jnp.where(key == 241, b1, 0.0) + jnp.where(key == 242, b2, 0.0)
+    taps = [(a, b) for a in range(3) for b in range(3)]
+    j = iota((40, KEYS), 0)
+    t = j // 4
+    a = (t >= 3).astype(jnp.int32) + (t >= 6).astype(jnp.int32)
+    code = jnp.where(j < 36, (t - 3 * a) * 24 + a * 4 + j % 4, -5000)
+    high_code, low_code, key = key_codes((40, KEYS), 1)
+    table = jnp.concatenate(
+        [w1_ref[a, b] for a, b in taps] + [bias_ref[...], jnp.zeros((3, channels), F32)], axis=0
     )
+    w_high, w_low = split(table)
+    bias_row = j == 36
+    over_rows = (((0,), (0,)), ((), ()))
     for out in range(WIN_OUT):
-        pick_high = jnp.where(code + 4 * out == high_code, 1.0, 0.0).astype(BF16)
-        pick_low = jnp.where(code + 4 * out == low_code, 1.0, 0.0).astype(BF16)
-        block = jnp.dot(w_high, pick_high, preferred_element_type=F32)
-        block += jnp.dot(w_low, pick_low, preferred_element_type=F32)
-        w1_out[out * channels : (out + 1) * channels, :] = (block + bias_part).astype(BF16)
+        pick_high = jnp.where((code + 4 * out == high_code) | (bias_row & (key == 240)), 1.0, 0.0).astype(BF16)
+        pick_low = jnp.where((code + 4 * out == low_code) | (bias_row & (key == 241)), 1.0, 0.0).astype(BF16)
+        block = lax.dot_general(w_high, pick_high, over_rows, preferred_element_type=F32)
+        block += lax.dot_general(w_low, pick_low, over_rows, preferred_element_type=F32)
+        w1_out[out * channels : (out + 1) * channels, :] = block.astype(BF16)
     spread = jnp.where(iota((channels, 8 * channels), 1) % channels == iota((channels, 8 * channels), 0), 1.0, 0.0)
-    halves = split(w2_ref[...] * TENDENCY)
+    halves = split(jnp.concatenate([w2_ref[a, b] for a, b in taps], axis=0) * TENDENCY)
     tables = [jnp.dot(h, spread.astype(BF16), preferred_element_type=F32).astype(BF16) for h in halves]
     m = iota((72, 8 * channels), 0)
     m_tap = (m >= 24).astype(jnp.int32) + (m >= 48).astype(jnp.int32)
@@ -100,10 +114,7 @@
             part = jnp.dot(pick, table, preferred_element_type=F32)
             total = total + jnp.where(k_row == m_row + tap_row, part, 0.0)
         full.append(total)
-    top = edge_ref[0]
-    bottom = edge_ref[1]
-    keep_top = 1.0 - top.astype(F32)
-    keep_bottom = 1.0 - bottom.astype(F32)
+    keep_top, keep_bottom = inside(strips)
     for part, total in enumerate(full):
         w2_out[0, part * 72 : (part + 1) * 72, :] = jnp.where(k_row < 3, total * keep_top, total).astype(BF16)
         w2_out[1, part * 72 : (part + 1) * 72, :] = jnp.where(k_row > 4, total * keep_bottom, total).astype(BF16)
@@ -196,26 +207,38 @@
     return moved(taps[0:third], 1) + taps[third : 2 * third] + moved(taps[2 * third :], -1)
 
 
+def inside(strips):
+    me = lax.axis_index("space")
+    return jnp.where(me == 0, 0.0, 1.0), jnp.where(me == strips - 1, 0.0, 1.0)
+
+
 def forecast_kernel(
-    edge_ref, head_ref, tail_ref, top_ref, bottom_ref, w1_ref, w2_ref, w2_last_ref, send_ref, done_ref, *, slots, parts_across
+    own_ref, core_got_ref, chip_got_ref, w1_ref, w2_ref, w2_last_ref, send_ref, done_ref, *, strips, slots, parts_across
 ):
     channels = w1_ref.shape[0] // WIN_OUT
-    pieces = head_ref.shape[1]
+    pieces = own_ref.shape[1]
     cols = pieces * LANES
-    keep_top = 1.0 - edge_ref[0].astype(F32)
-    keep_bottom = 1.0 - edge_ref[1].astype(F32)
+    keep_top, keep_bottom = inside(strips)
+    even = lax.axis_index("space") % 2 == 0
     blank = jnp.zeros((8, cols), F32)
 
-    def group_of(ref, index, half):
-        return jnp.concatenate([ref[index, p, 8 * half : 8 * half + 8, :] for p in range(pieces)], axis=1)
+    def own_group(index, g):
+        return jnp.concatenate([own_ref[index, p, 8 * g : 8 * g + 8, :] for p in range(pieces)], axis=1)
+
+    def got_group(above, index, g):
+        first, second = (chip_got_ref, core_got_ref) if above else (core_got_ref, chip_got_ref)
+        part = slice(8 * g, 8 * g + 8)
+        return jnp.concatenate(
+            [jnp.where(even, first[index, p, part, :], second[index, p, part, :]) for p in range(pieces)], axis=1
+        )
 
     def one_slot(slot, carry):
         frames = []
         for kind in range(2):
             index = kind * slots + slot
-            groups = []
-            for ref in (top_ref, head_ref, tail_ref, bottom_ref):
-                groups += [group_of(ref, index, 0), group_of(ref, index, 1)]
+            groups = [got_group(True, index, g) for g in range(2)]
+            groups += [own_group(index, g) for g in range(4)]
+            groups += [got_group(False, index, g) for g in range(2)]
             frames.append(groups + [blank])
         w1 = w1_ref[...]
         windows = hidden_pair(frames[0], frames[1], (0, 2, 4, 6), w1)
@@ -252,7 +275,7 @@
     for slot in range(slots + 1):
         if slot < slots:
             index = slots + slot
-            start = jnp.concatenate([group_of(ref, index, h) for ref in (head_ref, tail_ref) for h in range(2)], axis=0)
+            start = jnp.concatenate([own_group(index, g) for g in range(4)], axis=0)
             value = start - done_ref[slot - 1] if slot else start
         else:
             value = -done_ref[slot - 1]
@@ -283,47 +306,57 @@
     time = correlation.shape[1]
     parts_across = tm // rows
     width = cols // parts_across
-    me = lax.axis_index("space")
-    edges = jnp.stack([me == 0, me == strips - 1]).astype(jnp.int32)
-
+
+    hbm = pl.BlockSpec(memory_space=pltpu.HBM)
+    whole = jax.ShapeDtypeStruct((2 * slots, cols // LANES, rows * fields, LANES), F32)
     half = jax.ShapeDtypeStruct((2 * slots, cols // LANES, rows // 2 * fields, LANES), F32)
-    head, tail = pl.pallas_call(
-        pack_kernel, out_shape=(half, half), in_specs=[VMEM] * 2, out_specs=(VMEM, VMEM), compiler_params=params(), name="pack"
-    )(trajectory, increment)
-    top = lax.ppermute(tail, "space", [(i, i + 1) for i in range(strips - 1)])
-    bottom = lax.ppermute(head, "space", [(i + 1, i) for i in range(strips - 1)])
+    w1_taps = jnp.transpose(input_weight, (2, 3, 1, 0))
+    w2_taps = jnp.transpose(output_weight, (2, 3, 0, 1))
+    loaded = [
+        jax.ShapeDtypeStruct(shape, F32) for shape in (w1_taps.shape, (1, channels), w2_taps.shape, correlation.shape)
+    ]
+    strip = pltpu.VMEM(increment.shape, F32)
+    own, core, chip, w1_taps, bias_row, w2_taps, correlation = pl.pallas_call(
+        pack_kernel,
+        out_shape=(whole, half, half, *loaded),
+        in_specs=[hbm] * 6,
+        out_specs=(VMEM,) * 7,
+        scratch_shapes=[strip, strip, pltpu.SemaphoreType.DMA((6,))],
+        compiler_params=params(),
+        name="pack",
+    )(trajectory, increment, w1_taps, bias[None], w2_taps, correlation)
+
+    def swapped(value, first):
+        pairs = [(i, i + 1) for i in range(first, strips - 1, 2)]
+        return lax.ppermute(value, "space", pairs + [(j, i) for i, j in pairs])
+
+    chip_got = swapped(chip, 1)
+    core_got = swapped(core, 0)
 
     block_rows = (slots + 2) * fields
-    smem = pl.BlockSpec(memory_space=pltpu.SMEM)
     w1, w2, w2_last, mix = pl.pallas_call(
-        functools.partial(prepare_kernel, tm=tm, slots=slots),
+        functools.partial(prepare_kernel, strips=strips, slots=slots),
         out_shape=(
             jax.ShapeDtypeStruct((WIN_OUT * channels, KEYS), BF16),
             jax.ShapeDtypeStruct((3, 144, 8 * channels), BF16),
             jax.ShapeDtypeStruct((48, 4 * channels), BF16),
             jax.ShapeDtypeStruct((time * fields, tm * block_rows), F32),
         ),
-        in_specs=[smem] + [VMEM] * 4,
+        in_specs=[VMEM] * 4,
         out_specs=(VMEM,) * 4,
         compiler_params=params(),
         name="prepare",
-    )(
-        edges,
-        input_weight.reshape(channels, -1),
-        bias[:, None],
-        jnp.transpose(output_weight, (2, 3, 0, 1)).reshape(-1, channels),
-        correlation,
-    )
+    )(w1_taps, bias_row, w2_taps, correlation)
 
     send = pl.pallas_call(
-        functools.partial(forecast_kernel, slots=slots, parts_across=parts_across),
+        functools.partial(forecast_kernel, strips=strips, slots=slots, parts_across=parts_across),
         out_shape=jax.ShapeDtypeStruct((tm, block_rows, width), F32),
-        in_specs=[smem] + [VMEM] * 7,
+        in_specs=[VMEM] * 6,
         out_specs=VMEM,
         scratch_shapes=[pltpu.VMEM((slots, rows * fields, cols), F32)],
         compiler_params=params(),
         name="forecast",
-    )(edges, head, tail, top, bottom, w1, w2, w2_last)
+    )(own, core_got, chip_got, w1, w2, w2_last)
 
     blocks = lax.all_to_all(send, "tm", split_axis=0, concat_axis=0, tiled=True)
     mixed = pl.pallas_call(

time: 52 us -> 48.3 us (0.929)
  the two profiles are of different devices: /device:TPU:0 before, /device:TPU:4 now
where the time goes in v1:
time: 48.3 us; the launch traced here: 47.8 us
  blocking collectives  26.1 us (54%)
  Pallas kernels  9.41 us (19%)
  local copies, waits for them, and re-layouts  5.69 us (12%)
  waiting for transfers between devices  4.55 us (9%)
  starting transfers between devices  1.99 us (4%)
    all_to_all x1, blocking collectives, body(): blocks = lax.all_to_all(send, 'tm', split_axis=0, concat_axis=0, tiled=True)  15.1 us
    all_to_all x1, blocking collectives, body(): back = lax.all_to_all(mixed, 'tm', split_axis=0, concat_axis=0, tiled=True)  11.1 us
    pallas_call x1, Pallas kernels, body(): pl.pallas_call(functools.partial(forecast_kernel, strips=strips, slots=sl...  7.34 us
    unnamed x12, local copies, waits for them, and re-layouts  4.84 us
    ppermute x2, waiting for transfers between devices, swapped(): return lax.ppermute(value, 'space', pairs + [(j, i) for i, j in pairs])  4.55 us
    ppermute x2, starting transfers between devices, swapped(): return lax.ppermute(value, 'space', pairs + [(j, i) for i, j in pairs])  1.99 us
    pallas_call x1, Pallas kernels, body(): pl.pallas_call(functools.partial(prepare_kernel, strips=strips, slots=slo...  1.2 us
  transfers between devices with their start and end apart: 2, of which 1 were waited for; matrix products, arithmetic and copies ran while one was open for 0% of the time, Pallas kernels for 3%

profile of v1, /device:TPU:4, one launch (start us, length us, event | category | flops | bytes accessed | tf_op | source)
XLA Modules:
  0.0 47.8 jit_solution(14484642337584482116)
XLA Ops:
  0.0 0.0 copy-start.5
  0.0 0.7 %copy-done.5 = f32[32]{0:T(128)S(1)} copy-done((f32[32]{0:T(128)S(1)}, f32[32]{0:T(128)}, u32[]{:S(2)}) %copy-start.5) | copy-done | bytes 152
  0.7 0.0 copy-start
  0.7 0.9 %copy-done = f32[4,4,8,512]{3,2,1,0:T(8,128)S(1)} copy-done((f32[4,4,8,512]{3,2,1,0:T(8,128)S(1)}, f32[4,4,8,512]{3,2,1,0:T(8,128)}, u32[]{:S(2)}) %copy-start) | copy-done | bytes 262168
  1.6 0.0 copy-start.1
  1.6 0.9 %copy-done.1 = f32[4,4,8,512]{3,2,1,0:T(8,128)S(1)} copy-done((f32[4,4,8,512]{3,2,1,0:T(8,128)S(1)}, f32[4,4,8,512]{3,2,1,0:T(8,128)}, u32[]{:S(2)}) %copy-start.1) | copy-done | bytes 262168
  2.6 0.0 copy-start.2
  2.6 0.8 %copy-done.2 = f32[4,32,32]{2,1,0:T(8,128)S(1)} copy-done((f32[4,32,32]{2,1,0:T(8,128)S(1)}, f32[4,32,32]{2,1,0:T(8,128)}, u32[]{:S(2)}) %copy-start.2) | copy-done | bytes 16408
  3.4 0.0 copy-start.3
  3.4 0.7 %copy-done.3 = f32[32,4,3,3]{0,1,3,2:T(4,128)S(1)} copy-done((f32[32,4,3,3]{0,1,3,2:T(4,128)S(1)}, f32[32,4,3,3]{0,1,3,2:T(4,128)}, u32[]{:S(2)}) %copy-start.3) | copy-done | bytes 4632
  4.1 0.0 copy-start.4
  4.1 0.7 %copy-done.4 = f32[4,32,3,3]{1,0,3,2:T(4,128)S(1)} copy-done((f32[4,32,3,3]{1,0,3,2:T(4,128)S(1)}, f32[4,32,3,3]{1,0,3,2:T(4,128)}, u32[]{:S(2)}) %copy-start.4) | copy-done | bytes 4632
  4.8 0.5 pack.1
  5.3 0.1 collective-permute-start
  5.4 1.9 %collective-permute-start.1 = (f32[8,4,16,128]{3,2,1,0:T(8,128)S(1)}, f32[8,4,16,128]{3,2,1,0:T(8,128)S(1)}, u32[]{:S(2)}, u32[]{:S(2)}) collective-permute-start(f32[8,4,16,128]{3,2,1,0:T(8,128)S(1)} %get-tuple-element.23), channel_id=1, source_target_pairs={{1,2},{2,1},{5,6},{6,5},{9,10},{10,9},{13,14},{14,13},{17,18},{18,... | collective-permute-start | bytes 786440 | tf_op jit(solution)/shard_map/ppermute | solution.py:331
  7.3 1.2 %prepare.1 = (bf16[128,256]{1,0:T(8,128)(2,1)S(1)}, bf16[3,144,256]{2,1,0:T(8,128)(2,1)S(1)}, bf16[48,128]{1,0:T(8,128)(2,1)S(1)}, f32[128,192]{1,0:T(8,128)S(1)}) custom-call(f32[3,3,4,32]{3,2,1,0:T(4,128)S(1)} %get-tuple-element.16.w1_ref, f32[1,32]{1,0:T(1,128)S(1)} %get-tuple-element.17.bias_ref, f32[3,3,4,32]{3,2,1,0:T(4,128)S(1)} %get-tuple-element.18.w2_ref, ...), custom_call_target="tpu_custom_call" | custom-call | tf_op jit(solution)/shard_map/prepare/pallas_call | solution.py:337
  8.5 0.0 collective-permute-done.core_got_ref
  8.5 4.5 %collective-permute-done.1.chip_got_ref = f32[8,4,16,128]{3,2,1,0:T(8,128)S(1)} collective-permute-done((f32[8,4,16,128]{3,2,1,0:T(8,128)S(1)}, f32[8,4,16,128]{3,2,1,0:T(8,128)S(1)}, u32[]{:S(2)}, u32[]{:S(2)}) %collective-permute-start.1) | collective-permute-done | bytes 262176 | tf_op jit(solution)/shard_map/ppermute | solution.py:331
  13.1 7.3 %forecast.1 = f32[8,24,512]{2,1,0:T(8,128)S(1)} custom-call(f32[8,4,32,128]{3,2,1,0:T(8,128)S(1)} %get-tuple-element.21.own_ref, f32[8,4,16,128]{3,2,1,0:T(8,128)S(1)} %collective-permute-done.core_got_ref, f32[8,4,16,128]{3,2,1,0:T(8,128)S(1)} %collective-permute-done.1.chip_got_ref, bf16[128,256]{1,0:T(8,128)(2,1)S(1)} %get-tuple-element.24.w1_ref, ...), custom_call_target="tpu_custom_call" | custom-call | tf_op jit(solution)/shard_map/forecast/pallas_call | solution.py:351
  20.4 15.1 %all_to_all.10.block_ref = f32[8,24,512]{2,1,0:T(8,128)S(1)} all-to-all(f32[8,24,512]{2,1,0:T(8,128)S(1)} %forecast.1), channel_id=1, replica_groups=mesh['tm'=8,'space'=4] {'tm'}, dimensions={0} | all-to-all | bytes 786432 | tf_op jit(solution)/shard_map/all_to_all | solution.py:361
  35.5 0.4 mix.1
  35.9 11.1 %all_to_all.11 = f32[8,16,512]{2,1,0:T(8,128)S(1)} all-to-all(f32[8,16,512]{2,1,0:T(8,128)S(1)} %mix.1), channel_id=1, replica_groups=mesh['tm'=8,'space'=4] {'tm'}, dimensions={0} | all-to-all | bytes 524288 | tf_op jit(solution)/shard_map/all_to_all | solution.py:370
  47.0 0.9 %copy.8 = f32[8,16,512]{2,0,1:T(8,128)} copy(f32[8,16,512]{2,1,0:T(8,128)S(1)} %all_to_all.11) | data formatting | bytes 524288 | tf_op jit(solution)/shard_map/reshape | solution.py:371
Async XLA Ops:
  0.0 0.7 %copy-start.5 = (f32[32]{0:T(128)S(1)}, f32[32]{0:T(128)}, u32[]{:S(2)}) copy-start(f32[32]{0:T(128)} %param.9) | copy-start | bytes 388
  0.7 0.9 %copy-start = (f32[4,4,8,512]{3,2,1,0:T(8,128)S(1)}, f32[4,4,8,512]{3,2,1,0:T(8,128)}, u32[]{:S(2)}) copy-start(f32[4,4,8,512]{3,2,1,0:T(8,128)} %traj_hbm.1) | copy-start | bytes 786436
  1.6 0.9 %copy-start.1 = (f32[4,4,8,512]{3,2,1,0:T(8,128)S(1)}, f32[4,4,8,512]{3,2,1,0:T(8,128)}, u32[]{:S(2)}) copy-start(f32[4,4,8,512]{3,2,1,0:T(8,128)} %incr_hbm.1) | copy-start | bytes 786436
  2.6 0.8 %copy-start.2 = (f32[4,32,32]{2,1,0:T(8,128)S(1)}, f32[4,32,32]{2,1,0:T(8,128)}, u32[]{:S(2)}) copy-start(f32[4,32,32]{2,1,0:T(8,128)} %corr_hbm.1) | copy-start | bytes 49156
  3.4 0.7 %copy-start.3 = (f32[32,4,3,3]{0,1,3,2:T(4,128)S(1)}, f32[32,4,3,3]{0,1,3,2:T(4,128)}, u32[]{:S(2)}) copy-start(f32[32,4,3,3]{0,1,3,2:T(4,128)} %param.8) | copy-start | bytes 13828
  4.1 0.7 %copy-start.4 = (f32[4,32,3,3]{1,0,3,2:T(4,128)S(1)}, f32[4,32,3,3]{1,0,3,2:T(4,128)}, u32[]{:S(2)}) copy-start(f32[4,32,3,3]{1,0,3,2:T(4,128)} %param.10) | copy-start | bytes 13828
  5.3 3.2 %collective-permute-start = (f32[8,4,16,128]{3,2,1,0:T(8,128)S(1)}, f32[8,4,16,128]{3,2,1,0:T(8,128)S(1)}, u32[]{:S(2)}, u32[]{:S(2)}) collective-permute-start(f32[8,4,16,128]{3,2,1,0:T(8,128)S(1)} %get-tuple-element.22), channel_id=1, source_target_pairs={{0,1},{2,3},{1,0},{3,2},{4,5},{6,7},{5,4},{7,6},{8,9},{10,11},{9,8... | collective-permute-start | bytes 786440 | tf_op jit(solution)/shard_map/ppermute | solution.py:331
  5.4 7.7 %collective-permute-start.1 = (f32[8,4,16,128]{3,2,1,0:T(8,128)S(1)}, f32[8,4,16,128]{3,2,1,0:T(8,128)S(1)}, u32[]{:S(2)}, u32[]{:S(2)}) collective-permute-start(f32[8,4,16,128]{3,2,1,0:T(8,128)S(1)} %get-tuple-element.23), channel_id=1, source_target_pairs={{1,2},{2,1},{5,6},{6,5},{9,10},{10,9},{13,14},{14,13},{17,18},{18,... | collective-permute-start | bytes 786440 | tf_op jit(solution)/shard_map/ppermute | solution.py:331

commit v2 on v1

--- a/solution.py
+++ b/solution.py
@@ -324,7 +324,7 @@
         scratch_shapes=[strip, strip, pltpu.SemaphoreType.DMA((6,))],
         compiler_params=params(),
         name="pack",
-    )(trajectory, increment, w1_taps, bias[None], w2_taps, correlation)
+    )(*[pltpu.with_memory_space_constraint(x, pltpu.HBM) for x in (trajectory, increment, w1_taps, bias[None], w2_taps, correlation)])
 
     def swapped(value, first):
         pairs = [(i, i + 1) for i in range(first, strips - 1, 2)]

time: 48.3 us -> 44 us (0.911)
  local copies, waits for them, and re-layouts: 5.69 us -> 0.86 us
  Pallas kernels: 9.41 us -> 10.2 us
    unnamed x12 -> x0, local copies, waits for them, and re-layouts: 4.84 us -> none
    pallas_call x1, Pallas kernels: 0.47 us -> 1.25 us  [body(): pl.pallas_call(pack_kernel, out_shape=(whole, half, half, *loaded), in_sp...]
where the time goes in v2:
time: 44 us; the launch traced here: 43.8 us
  blocking collectives  26.1 us (59%)
  Pallas kernels  10.2 us (23%)
  waiting for transfers between devices  4.54 us (10%)
  starting transfers between devices  1.99 us (5%)
  local copies, waits for them, and re-layouts  0.86 us (2%)
    all_to_all x1, blocking collectives, body(): blocks = lax.all_to_all(send, 'tm', split_axis=0, concat_axis=0, tiled=True)  15.1 us
    all_to_all x1, blocking collectives, body(): back = lax.all_to_all(mixed, 'tm', split_axis=0, concat_axis=0, tiled=True)  11.1 us
    pallas_call x1, Pallas kernels, body(): pl.pallas_call(functools.partial(forecast_kernel, strips=strips, slots=sl...  7.35 us
    ppermute x2, waiting for transfers between devices, swapped(): return lax.ppermute(value, 'space', pairs + [(j, i) for i, j in pairs])  4.54 us
    ppermute x2, starting transfers between devices, swapped(): return lax.ppermute(value, 'space', pairs + [(j, i) for i, j in pairs])  1.99 us
    pallas_call x1, Pallas kernels, body(): pl.pallas_call(pack_kernel, out_shape=(whole, half, half, *loaded), in_sp...  1.25 us
    pallas_call x1, Pallas kernels, body(): pl.pallas_call(functools.partial(prepare_kernel, strips=strips, slots=slo...  1.21 us
  transfers between devices with their start and end apart: 2, of which 1 were waited for; matrix products, arithmetic and copies ran while one was open for 0% of the time, Pallas kernels for 3%

profile of v2, /device:TPU:4, one launch (start us, length us, event | category | flops | bytes accessed | tf_op | source)
XLA Modules:
  0.0 43.8 jit_solution(16661393963457677014)
XLA Ops:
  0.0 1.2 %pack.1 = (f32[8,4,32,128]{3,2,1,0:T(8,128)S(1)}, f32[8,4,16,128]{3,2,1,0:T(8,128)S(1)}, f32[8,4,16,128]{3,2,1,0:T(8,128)S(1)}, f32[3,3,4,32]{3,2,1,0:T(4,128)S(...) custom-call(f32[4,4,8,512]{3,2,1,0:T(8,128)} %traj_hbm.1, ...), custom_call_target="tpu_custom_call" | custom-call | tf_op jit(solution)/shard_map/pack/pallas_call | solution.py:319
  1.3 0.1 collective-permute-start
  1.3 1.9 %collective-permute-start.1 = (f32[8,4,16,128]{3,2,1,0:T(8,128)S(1)}, f32[8,4,16,128]{3,2,1,0:T(8,128)S(1)}, u32[]{:S(2)}, u32[]{:S(2)}) collective-permute-start(f32[8,4,16,128]{3,2,1,0:T(8,128)S(1)} %get-tuple-element.23), channel_id=1, source_target_pairs={{1,2},{2,1},{5,6},{6,5},{9,10},{10,9},{13,14},{14,13},{17,18},{18,... | collective-permute-start | bytes 786440 | tf_op jit(solution)/shard_map/ppermute | solution.py:331
  3.3 1.2 %prepare.1 = (bf16[128,256]{1,0:T(8,128)(2,1)S(1)}, bf16[3,144,256]{2,1,0:T(8,128)(2,1)S(1)}, bf16[48,128]{1,0:T(8,128)(2,1)S(1)}, f32[128,192]{1,0:T(8,128)S(1)}) custom-call(f32[3,3,4,32]{3,2,1,0:T(4,128)S(1)} %get-tuple-element.16.w1_ref, f32[1,32]{1,0:T(1,128)S(1)} %get-tuple-element.17.bias_ref, f32[3,3,4,32]{3,2,1,0:T(4,128)S(1)} %get-tuple-element.18.w2_ref, ...), custom_call_target="tpu_custom_call" | custom-call | tf_op jit(solution)/shard_map/prepare/pallas_call | solution.py:337
  4.5 0.0 collective-permute-done.core_got_ref
  4.5 4.5 %collective-permute-done.1.chip_got_ref = f32[8,4,16,128]{3,2,1,0:T(8,128)S(1)} collective-permute-done((f32[8,4,16,128]{3,2,1,0:T(8,128)S(1)}, f32[8,4,16,128]{3,2,1,0:T(8,128)S(1)}, u32[]{:S(2)}, u32[]{:S(2)}) %collective-permute-start.1) | collective-permute-done | bytes 262176 | tf_op jit(solution)/shard_map/ppermute | solution.py:331
  9.0 7.3 %forecast.1 = f32[8,24,512]{2,1,0:T(8,128)S(1)} custom-call(f32[8,4,32,128]{3,2,1,0:T(8,128)S(1)} %get-tuple-element.21.own_ref, f32[8,4,16,128]{3,2,1,0:T(8,128)S(1)} %collective-permute-done.core_got_ref, f32[8,4,16,128]{3,2,1,0:T(8,128)S(1)} %collective-permute-done.1.chip_got_ref, bf16[128,256]{1,0:T(8,128)(2,1)S(1)} %get-tuple-element.24.w1_ref, ...), custom_call_target="tpu_custom_call" | custom-call | tf_op jit(solution)/shard_map/forecast/pallas_call | solution.py:351
  16.4 15.1 %all_to_all.10.block_ref = f32[8,24,512]{2,1,0:T(8,128)S(1)} all-to-all(f32[8,24,512]{2,1,0:T(8,128)S(1)} %forecast.1), channel_id=1, replica_groups=mesh['tm'=8,'space'=4] {'tm'}, dimensions={0} | all-to-all | bytes 786432 | tf_op jit(solution)/shard_map/all_to_all | solution.py:361
  31.4 0.4 mix.1
  31.8 11.1 %all_to_all.11 = f32[8,16,512]{2,1,0:T(8,128)S(1)} all-to-all(f32[8,16,512]{2,1,0:T(8,128)S(1)} %mix.1), channel_id=1, replica_groups=mesh['tm'=8,'space'=4] {'tm'}, dimensions={0} | all-to-all | bytes 524288 | tf_op jit(solution)/shard_map/all_to_all | solution.py:370
  42.9 0.9 %copy.8 = f32[8,16,512]{2,0,1:T(8,128)} copy(f32[8,16,512]{2,1,0:T(8,128)S(1)} %all_to_all.11) | data formatting | bytes 524288 | tf_op jit(solution)/shard_map/reshape | solution.py:371
Async XLA Ops:
  1.3 3.2 %collective-permute-start = (f32[8,4,16,128]{3,2,1,0:T(8,128)S(1)}, f32[8,4,16,128]{3,2,1,0:T(8,128)S(1)}, u32[]{:S(2)}, u32[]{:S(2)}) collective-permute-start(f32[8,4,16,128]{3,2,1,0:T(8,128)S(1)} %get-tuple-element.22), channel_id=1, source_target_pairs={{0,1},{2,3},{1,0},{3,2},{4,5},{6,7},{5,4},{7,6},{8,9},{10,11},{9,8... | collective-permute-start | bytes 786440 | tf_op jit(solution)/shard_map/ppermute | solution.py:331
  1.3 7.7 %collective-permute-start.1 = (f32[8,4,16,128]{3,2,1,0:T(8,128)S(1)}, f32[8,4,16,128]{3,2,1,0:T(8,128)S(1)}, u32[]{:S(2)}, u32[]{:S(2)}) collective-permute-start(f32[8,4,16,128]{3,2,1,0:T(8,128)S(1)} %get-tuple-element.23), channel_id=1, source_target_pairs={{1,2},{2,1},{5,6},{6,5},{9,10},{10,9},{13,14},{14,13},{17,18},{18,... | collective-permute-start | bytes 786440 | tf_op jit(solution)/shard_map/ppermute | solution.py:331

commit v3 on v2

v3 whole, which is shorter than its diff:
```python
import functools

import jax
import jax.numpy as jnp
from jax import lax
from jax.experimental import pallas as pl
from jax.experimental.pallas import tpu as pltpu
from jax.sharding import PartitionSpec as P

STEPS = 2
TENDENCY = 0.5
HALO = 2 * STEPS
F32 = jnp.float32
BF16 = jnp.bfloat16
EXACT = lax.Precision.HIGHEST
VMEM = pl.BlockSpec(memory_space=pltpu.VMEM)

WIN_OUT = 4
LANES = 128
KEYS = 256
HALF_KEYS = 160


def iota(shape, dim):
    return lax.broadcasted_iota(jnp.int32, shape, dim)


def split(value):
    high = value.astype(BF16)
    return high, (value - high.astype(F32)).astype(BF16)


def pack_kernel(
    traj_hbm, incr_hbm, w1_hbm, bias_hbm, w2_hbm, corr_hbm,
    own_ref, core_ref, chip_ref, w1_ref, bias_ref, w2_ref, corr_ref,
    traj_ref, incr_ref, sems,
):
    pairs = (
        (traj_hbm, traj_ref), (incr_hbm, incr_ref), (w1_hbm, w1_ref), (bias_hbm, bias_ref), (w2_hbm, w2_ref), (corr_hbm, corr_ref)
    )
    copies = [pltpu.make_async_copy(src, dst, sems.at[n]) for n, (src, dst) in enumerate(pairs)]
    for copy in copies:
        copy.start()
    slots, fields, rows, _ = traj_ref.shape
    half = rows // 2 * fields
    odd = lax.axis_index("space") % 2
    core_half = pl.ds(pl.multiple_of((1 - odd) * half, half), half)
    chip_half = pl.ds(pl.multiple_of(odd * half, half), half)
    for kind, ref in enumerate((traj_ref, incr_ref)):
        copies[kind].wait()
        for slot in range(slots):
            index = kind * slots + slot
            for piece in range(own_ref.shape[1]):
                for f in range(fields):
                    own_ref[index, piece, pl.ds(f, rows, stride=fields), :] = ref[
                        slot, f, :, piece * LANES : (piece + 1) * LANES
                    ]
                core_ref[index, piece] = own_ref[index, piece, core_half, :]
                chip_ref[index, piece] = own_ref[index, piece, chip_half, :]
    for copy in copies[2:]:
        copy.wait()


def key_codes(shape, dim):
    key = iota(shape, dim)
    none = -1000
    q = key - 16
    front_high = (q // 32) * 24 + q % 16
    q = key - 112
    front_low = (q // 16) * 24 + q % 16
    q = key - 160
    back_high = (q // 16) * 24 + 16 + q % 8
    q = key - 208
    back_low = (q // 16) * 24 + 16 + q % 8
    high = jnp.where((key >= 16) & (key < 112), front_high, jnp.where((key >= 160) & (key < 208), back_high, none))
    low = jnp.where((key >= 112) & (key < 160), front_low, jnp.where(key >= 208, back_low, none))
    return high, low, key


def prepare_kernel(w1_ref, bias_ref, w2_ref, corr_ref, w1_out, w2_out, w2_half, mix_out, *, strips, slots):
    fields = w1_ref.shape[2]
    channels = w1_ref.shape[3]
    time = corr_ref.shape[1]
    taps = [(a, b) for a in range(3) for b in range(3)]
    j = iota((40, KEYS), 0)
    t = j // 4
    a = (t >= 3).astype(jnp.int32) + (t >= 6).astype(jnp.int32)
    code = jnp.where(j < 36, (t - 3 * a) * 24 + a * 4 + j % 4, -5000)
    high_code, low_code, key = key_codes((40, KEYS), 1)
    table = jnp.concatenate(
        [w1_ref[a, b] for a, b in taps] + [bias_ref[...], jnp.zeros((3, channels), F32)], axis=0
    )
    w_high, w_low = split(table)
    bias_row = j == 36
    over_rows = (((0,), (0,)), ((), ()))
    for out in range(WIN_OUT):
        pick_high = jnp.where((code + 4 * out == high_code) | (bias_row & (key == 0)), 1.0, 0.0).astype(BF16)
        pick_low = jnp.where((code + 4 * out == low_code) | (bias_row & (key == 1)), 1.0, 0.0).astype(BF16)
        block = lax.dot_general(w_high, pick_high, over_rows, preferred_element_type=F32)
        block += lax.dot_general(w_low, pick_low, over_rows, preferred_element_type=F32)
        w1_out[out * channels : (out + 1) * channels, :] = block.astype(BF16)
    keys = WIN_OUT * channels
    spread = jnp.where(iota((channels, keys), 1) % channels == iota((channels, keys), 0), 1.0, 0.0).astype(BF16)
    halves = split(jnp.concatenate([w2_ref[a, b] for a, b in taps], axis=0) * TENDENCY)
    tables = [jnp.dot(h, spread, preferred_element_type=F32).astype(BF16) for h in halves]
    m = iota((72, keys), 0)
    m_row = (m - jnp.where(m >= 48, 48, jnp.where(m >= 24, 24, 0))) // 4
    k_row = iota((72, keys), 1) // channels
    mj = iota((72, 36), 0)
    mj_tap = jnp.where(mj >= 48, 2, jnp.where(mj >= 24, 1, 0))
    full = []
    for table in tables:
        total = jnp.zeros((72, keys), F32)
        for tap_row in range(3):
            pick = jnp.where(iota((72, 36), 1) == tap_row * 12 + mj_tap * 4 + mj % 4, 1.0, 0.0).astype(BF16)
            part = jnp.dot(pick, table, preferred_element_type=F32)
            total = total + jnp.where(k_row == m_row - 2 + tap_row, part, 0.0)
        full.append(total)
    even, keep = chip_side(strips)
    outside = (
        None,
        (even & (k_row < 3)) | (~even & (k_row > 0)),
        (even & (k_row < 1)) | (~even & (k_row > 2)),
    )
    for form, rows_out in enumerate(outside):
        high, low = [t if rows_out is None else jnp.where(rows_out, t * keep, t) for t in full]
        w2_out[form, 0:72, 0:keys] = high.astype(BF16)
        w2_out[form, 0:72, keys:] = high.astype(BF16)
        w2_out[form, 72:, 0:keys] = low.astype(BF16)
        w2_out[form, 72:, keys:] = jnp.zeros((72, keys), BF16)
    short = keys // 2
    high, low = [
        jnp.concatenate([t[24 * tap : 24 * tap + 16, 0:short] for tap in range(3)], axis=0).astype(BF16) for t in full
    ]
    w2_half[0:48, :] = jnp.concatenate([high, high], axis=1)
    w2_half[48:, :] = jnp.concatenate([low, jnp.zeros((48, short), BF16)], axis=1)
    keys = mix_out.shape[1]
    block = (slots + 2) * fields
    key = iota((time, keys), 1)
    sender = key // block
    row = key - sender * block
    slot = slots * sender + row // fields
    valid = row < (slots + 1) * fields
    pick = jnp.where((iota((time, keys), 0) == slot) & valid, 1.0, 0.0)
    total = jnp.zeros(mix_out.shape, F32)
    wide = (time * fields, time)
    repeat = jnp.where(iota(wide, 0) // fields == iota(wide, 1), 1.0, 0.0)
    to_field = iota(mix_out.shape, 0) % fields
    from_field = iota(mix_out.shape, 1) % fields
    for f in range(fields):
        part = jnp.dot(corr_ref[f], pick, precision=EXACT, preferred_element_type=F32)
        part = jnp.dot(repeat, part, precision=EXACT, preferred_element_type=F32)
        total = jnp.where((to_field == f) & (from_field == f), part, total)
    mix_out[...] = total


def moved(value, shift):
    if shift == 0:
        return value
    cols = value.shape[1]
    column = iota(value.shape, 1)
    turned = pltpu.roll(value, shift % cols, 1)
    outside = column == (0 if shift > 0 else cols - 1)
    return jnp.where(outside, 0.0, turned)


def window_keys(groups, bias):
    cols = groups[0].shape[1]
    front_high, front_low, back_high, back_low = [], [], [], []
    for tap in range(3):
        value = moved(jnp.concatenate(groups[:2], axis=0), 1 - tap)
        high, low = split(value)
        front_high += [high, low]
        front_low.append(high)
        if len(groups) == 3:
            value = moved(groups[2], 1 - tap)
            high = value.astype(BF16).astype(F32)
            both = jnp.concatenate([high, value - high], axis=0).astype(BF16)
            back_high.append(both)
            back_low.append(both)
    first = jnp.full((16, cols), 1.0 if bias else 0.0, BF16)
    return jnp.concatenate([first] + front_high + front_low + back_high + back_low, axis=0)


def hidden_pair(state_groups, tangent_groups, w1_ref):
    rows, keys = w1_ref.shape
    if len(state_groups) == 2:
        rows, keys = rows // 2, HALF_KEYS
    w1 = w1_ref[0:rows, 0:keys]
    z = jnp.dot(w1, window_keys(state_groups, True), preferred_element_type=F32)
    dz = jnp.dot(w1, window_keys(tangent_groups, False), preferred_element_type=F32)
    h = jnp.tanh(z)
    return h, (1.0 - h * h) * dz


def spread_hidden(hidden, weight):
    taps = jnp.dot(weight, jnp.concatenate(split(hidden), axis=0), preferred_element_type=F32)
    half = taps.shape[0] // 2
    taps = taps[:half] + taps[half:]
    third = half // 3
    total = moved(taps[0:third], 1) + taps[third : 2 * third] + moved(taps[2 * third :], -1)
    return [total[g : g + 8] for g in range(0, third, 8)]


def chip_side(strips):
    me = lax.axis_index("space")
    even = me % 2 == 0
    return even, jnp.where((me == 0) | (me == strips - 1), 0.0, 1.0)


def read_group(ref, index, g):
    pieces = ref.shape[1]
    return jnp.concatenate([ref[index, p, 8 * g : 8 * g + 8, :] for p in range(pieces)], axis=1)


def inner_kernel(own_ref, core_got_ref, w1_ref, w2_ref, w2_half_ref, kept_ref, *, strips, slots):
    even, _ = chip_side(strips)

    def pick(if_even, if_odd):
        return jnp.where(even, if_even, if_odd)

    for slot in range(slots):
        line, ends = [], []
        for index in (slot, slots + slot):
            own = [read_group(own_ref, index, g) for g in range(4)]
            core = [read_group(core_got_ref, index, g) for g in range(2)]
            line.append([pick(a, b) for a, b in zip(own + core[:1], core[1:] + own)])
            ends.append(core)
        first = hidden_pair(line[0][0:3], line[1][0:3], w1_ref)
        second = hidden_pair(line[0][2:5], line[1][2:5], w1_ref)
        last = hidden_pair(ends[0], ends[1], w1_ref)
        moved_on = []
        for kind in range(2):
            a = spread_hidden(first[kind], w2_ref[0])
            b = spread_hidden(second[kind], w2_ref[0])
            c = spread_hidden(last[kind], w2_half_ref[...])
            added = [a[0] + pick(0.0, c[1]), a[1], a[2] + b[0], b[1], b[2] + pick(c[0], 0.0)]
            moved_on.append([x + y for x, y in zip(line[kind], added)])
        s, t = moved_on
        outer = hidden_pair(
            [pick(a, b) for a, b in zip(s[2:5], s[0:3])], [pick(a, b) for a, b in zip(t[2:5], t[0:3])], w1_ref
        )
        middle = hidden_pair(
            [pick(a, b) for a, b in zip(s[1:3], s[2:4])], [pick(a, b) for a, b in zip(t[1:3], t[2:4])], w1_ref
        )
        u = spread_hidden(outer[1], w2_ref[0])
        v = spread_hidden(middle[1], w2_half_ref[...])
        kept = [
            pick(t[3], t[1]) + u[1],
            t[2] + pick(u[0], u[2]) + pick(v[1], v[0]),
            pick(t[1], t[3]) + pick(v[0], v[1]),
            pick(s[0], s[4]),
            pick(t[0], t[4]),
            pick(s[1], s[3]),
            pick(t[1], t[3]),
        ]
        for g, value in enumerate(kept):
            kept_ref[slot, 8 * g : 8 * g + 8, :] = value


def outer_kernel(own_ref, chip_got_ref, kept_ref, w1_ref, w2_ref, send_ref, *, strips, slots, parts_across):
    even, keep = chip_side(strips)
    cols = kept_ref.shape[2]
    width = cols // parts_across
    fields, rows = 4, 8

    def pick(if_even, if_odd):
        return jnp.where(even, if_even, if_odd)

    def in_order(values):
        return [pick(a, b) for a, b in zip(values, values[::-1])]

    def send(value, slot):
        for y in range(rows):
            for block in range(parts_across):
                send_ref[y * parts_across + block, slot * fields : (slot + 1) * fields, :] = value[
                    y * fields : (y + 1) * fields, block * width : (block + 1) * width
                ]

    def start(slot):
        return jnp.concatenate([read_group(own_ref, slots + slot, g) for g in range(4)], axis=0)

    send(start(0), 0)
    for slot in range(slots):
        f_outer, f_middle, f_inner, s_near, t_near, s_next, t_next = [
            kept_ref[slot, 8 * g : 8 * g + 8, :] for g in range(7)
        ]
        frames = []
        for index in (slot, slots + slot):
            chip = [read_group(chip_got_ref, index, g) for g in range(2)]
            own = [read_group(own_ref, index, g) for g in (0, 3)]
            frames.append([pick(chip[0], own[1]), pick(chip[1], chip[0]), pick(own[0], chip[1])])
        pair = hidden_pair(frames[0], frames[1], w1_ref)
        state, tangent = [], []
        for kind, (near, result) in enumerate(((s_near, state), (t_near, tangent))):
            w = spread_hidden(pair[kind], w2_ref[1])
            result += [(frames[kind][1] + w[1]) * keep, near + pick(w[2], w[0])]
        pair = hidden_pair(in_order(state + [s_next]), in_order(tangent + [t_next]), w1_ref)
        x = spread_hidden(pair[1], w2_ref[2])
        ends = [tangent[1] + x[1], f_inner + pick(x[2], x[0]), f_middle, f_outer]
        final = jnp.concatenate(in_order(ends), axis=0)
        send(start(slot + 1) - final if slot < slots - 1 else -final, slot + 1)
    send_ref[:, (slots + 1) * fields :, :] = jnp.zeros((rows * parts_across, fields, width), F32)


def mix_kernel(mix_ref, block_ref, out_ref):
    count, rows, width = block_ref.shape
    keys = block_ref[...].reshape(count * rows, width)
    out = jnp.dot(mix_ref[...], keys, precision=EXACT, preferred_element_type=F32)
    out_ref[...] = out.reshape(out_ref.shape)


def params():
    return pltpu.CompilerParams(vmem_limit_bytes=24 * 1024 * 1024)


def body(increment, trajectory, input_weight, bias, output_weight, correlation):
    slots, fields, rows, cols = increment.shape
    channels = input_weight.shape[0]
    tm = lax.axis_size("tm")
    strips = lax.axis_size("space")
    time = correlation.shape[1]
    parts_across = tm // rows
    width = cols // parts_across

    hbm = pl.BlockSpec(memory_space=pltpu.HBM)
    whole = jax.ShapeDtypeStruct((2 * slots, cols // LANES, rows * fields, LANES), F32)
    half = jax.ShapeDtypeStruct((2 * slots, cols // LANES, rows // 2 * fields, LANES), F32)
    w1_taps = jnp.transpose(input_weight, (2, 3, 1, 0))
    w2_taps = jnp.transpose(output_weight, (2, 3, 0, 1))
    loaded = [
        jax.ShapeDtypeStruct(shape, F32) for shape in (w1_taps.shape, (1, channels), w2_taps.shape, correlation.shape)
    ]
    strip = pltpu.VMEM(increment.shape, F32)
    own, core, chip, w1_taps, bias_row, w2_taps, correlation = pl.pallas_call(
        pack_kernel,
        out_shape=(whole, half, half, *loaded),
        in_specs=[hbm] * 6,
        out_specs=(VMEM,) * 7,
        scratch_shapes=[strip, strip, pltpu.SemaphoreType.DMA((6,))],
        compiler_params=params(),
        name="pack",
    )(*[pltpu.with_memory_space_constraint(x, pltpu.HBM) for x in (trajectory, increment, w1_taps, bias[None], w2_taps, correlation)])

    def swapped(value, first):
        pairs = [(i, i + 1) for i in range(first, strips - 1, 2)]
        return lax.ppermute(value, "space", pairs + [(j, i) for i, j in pairs])

    chip_got = swapped(chip, 1)
    core_got = swapped(core, 0)

    block_rows = (slots + 2) * fields
    w1, w2, w2_half, mix = pl.pallas_call(
        functools.partial(prepare_kernel, strips=strips, slots=slots),
        out_shape=(
            jax.ShapeDtypeStruct((WIN_OUT * channels, KEYS), BF16),
            jax.ShapeDtypeStruct((3, 144, 2 * WIN_OUT * channels), BF16),
            jax.ShapeDtypeStruct((96, WIN_OUT * channels), BF16),
            jax.ShapeDtypeStruct((time * fields, tm * block_rows), F32),
        ),
        in_specs=[VMEM] * 4,
        out_specs=(VMEM,) * 4,
        compiler_params=params(),
        name="prepare",
    )(w1_taps, bias_row, w2_taps, correlation)

    kept = pl.pallas_call(
        functools.partial(inner_kernel, strips=strips, slots=slots),
        out_shape=jax.ShapeDtypeStruct((slots, 56, cols), F32),
        in_specs=[VMEM] * 5,
        out_specs=VMEM,
        compiler_params=params(),
        name="inner",
    )(own, core_got, w1, w2, w2_half)

    send = pl.pallas_call(
        functools.partial(outer_kernel, strips=strips, slots=slots, parts_across=parts_across),
        out_shape=jax.ShapeDtypeStruct((tm, block_rows, width), F32),
        in_specs=[VMEM] * 5,
        out_specs=VMEM,
        compiler_params=params(),
        name="outer",
    )(own, chip_got, kept, w1, w2)

    blocks = lax.all_to_all(send, "tm", split_axis=0, concat_axis=0, tiled=True)
    mixed = pl.pallas_call(
        mix_kernel,
        out_shape=jax.ShapeDtypeStruct((tm, slots * fields, width), F32),
        in_specs=[VMEM] * 2,
        out_specs=VMEM,
        compiler_params=params(),
        name="mix",
    )(mix, blocks)
    back = lax.all_to_all(mixed, "tm", split_axis=0, concat_axis=0, tiled=True)
    back = back.reshape(rows, parts_across, slots, fields, width)
    return jnp.transpose(back, (2, 3, 0, 1, 4)).reshape(slots, fields, rows, cols)


def solution(mesh):
    placed = (P("tm", None, "space", None), P("tm", None, "space", None), P(), P(), P(), P())
    return jax.shard_map(
        body, mesh=mesh, in_specs=placed, out_specs=P("tm", None, "space", None), check_vma=False
    )
```

time: 44 us -> 45.9 us (1.043)
  the two profiles are of different devices: /device:TPU:4 before, /device:TPU:0 now
where the time goes in v3:
time: 45.9 us; the launch traced here: 45.7 us
  blocking collectives  32.1 us (70%)
  Pallas kernels  11.5 us (25%)
  starting transfers between devices  1.18 us (3%)
  local copies, waits for them, and re-layouts  0.86 us (2%)
    all_to_all x1, blocking collectives, body(): blocks = lax.all_to_all(send, 'tm', split_axis=0, concat_axis=0, tiled=True)  17.6 us
    all_to_all x1, blocking collectives, body(): back = lax.all_to_all(mixed, 'tm', split_axis=0, concat_axis=0, tiled=True)  14.5 us
    pallas_call x1, Pallas kernels, body(): pl.pallas_call(functools.partial(inner_kernel, strips=strips, slots=slots...  4.97 us
    pallas_call x1, Pallas kernels, body(): pl.pallas_call(functools.partial(outer_kernel, strips=strips, slots=slots...  3.71 us
    pallas_call x1, Pallas kernels, body(): pl.pallas_call(pack_kernel, out_shape=(whole, half, half, *loaded), in_sp...  1.25 us
    pallas_call x1, Pallas kernels, body(): pl.pallas_call(functools.partial(prepare_kernel, strips=strips, slots=slo...  1.21 us
    ppermute x2, starting transfers between devices, swapped(): return lax.ppermute(value, 'space', pairs + [(j, i) for i, j in pairs])  1.18 us
  transfers between devices with their start and end apart: 2, of which 0 were waited for; matrix products, arithmetic and copies ran while one was open for 0% of the time, Pallas kernels for 14%

profile of v3, /device:TPU:0, one launch (start us, length us, event | category | flops | bytes accessed | tf_op | source)
XLA Modules:
  0.0 45.7 jit_solution(12719492928050600520)
XLA Ops:
  0.0 1.2 %pack.1 = (f32[8,4,32,128]{3,2,1,0:T(8,128)S(1)}, f32[8,4,16,128]{3,2,1,0:T(8,128)S(1)}, f32[8,4,16,128]{3,2,1,0:T(8,128)S(1)}, f32[3,3,4,32]{3,2,1,0:T(4,128)S(...) custom-call(f32[4,4,8,512]{3,2,1,0:T(8,128)} %traj_hbm.1, ...), custom_call_target="tpu_custom_call" | custom-call | tf_op jit(solution)/shard_map/pack/pallas_call | solution.py:335
  1.3 0.5 %collective-permute-start.1 = (f32[8,4,16,128]{3,2,1,0:T(8,128)S(1)}, f32[8,4,16,128]{3,2,1,0:T(8,128)S(1)}, u32[]{:S(2)}, u32[]{:S(2)}) collective-permute-start(f32[8,4,16,128]{3,2,1,0:T(8,128)S(1)} %get-tuple-element.23), channel_id=1, source_target_pairs={{0,1},{2,3},{1,0},{3,2},{4,5},{6,7},{5,4},{7,6},{8,9},{10,11},{9,8... | collective-permute-start | bytes 786440 | tf_op jit(solution)/shard_map/ppermute | solution.py:347
  1.8 0.7 %collective-permute-start = (f32[8,4,16,128]{3,2,1,0:T(8,128)S(1)}, f32[8,4,16,128]{3,2,1,0:T(8,128)S(1)}, u32[]{:S(2)}, u32[]{:S(2)}) collective-permute-start(f32[8,4,16,128]{3,2,1,0:T(8,128)S(1)} %get-tuple-element.22), channel_id=1, source_target_pairs={{1,2},{2,1},{5,6},{6,5},{9,10},{10,9},{13,14},{14,13},{17,18},{18,... | collective-permute-start | bytes 786440 | tf_op jit(solution)/shard_map/ppermute | solution.py:347
  2.4 1.2 %prepare.1 = (bf16[128,256]{1,0:T(8,128)(2,1)S(1)}, bf16[3,144,256]{2,1,0:T(8,128)(2,1)S(1)}, bf16[96,128]{1,0:T(8,128)(2,1)S(1)}, f32[128,192]{1,0:T(8,128)S(1)}) custom-call(f32[3,3,4,32]{3,2,1,0:T(4,128)S(1)} %get-tuple-element.16.w1_ref, f32[1,32]{1,0:T(1,128)S(1)} %get-tuple-element.17.bias_ref, f32[3,3,4,32]{3,2,1,0:T(4,128)S(1)} %get-tuple-element.18.w2_ref, ...), custom_call_target="tpu_custom_call" | custom-call | tf_op jit(solution)/shard_map/prepare/pallas_call | solution.py:353
  3.7 0.0 collective-permute-done.1.core_got_ref
  3.7 5.0 %inner.1.kept_ref = f32[4,56,512]{2,1,0:T(8,128)S(1)} custom-call(f32[8,4,32,128]{3,2,1,0:T(8,128)S(1)} %get-tuple-element.21.own_ref, f32[8,4,16,128]{3,2,1,0:T(8,128)S(1)} %collective-permute-done.1.core_got_ref, bf16[128,256]{1,0:T(8,128)(2,1)S(1)} %get-tuple-element.24.w1_ref, bf16[3,144,256]{2,1,0:T(8,128)(2,1)S(1)} %get-tuple-element.25.w2_ref, ...), custom_call_target="tpu_custom_call" | custom-call | tf_op jit(solution)/shard_map/inner/pallas_call | solution.py:367
  8.7 0.0 collective-permute-done.chip_got_ref
  8.7 3.7 %outer.1 = f32[8,24,512]{2,1,0:T(8,128)S(1)} custom-call(f32[8,4,32,128]{3,2,1,0:T(8,128)S(1)} %get-tuple-element.21.own_ref, f32[8,4,16,128]{3,2,1,0:T(8,128)S(1)} %collective-permute-done.chip_got_ref, f32[4,56,512]{2,1,0:T(8,128)S(1)} %inner.1.kept_ref, bf16[128,256]{1,0:T(8,128)(2,1)S(1)} %get-tuple-element.24.w1_ref, ...), custom_call_target="tpu_custom_call" | custom-call | tf_op jit(solution)/shard_map/outer/pallas_call | solution.py:376
  12.4 17.6 %all_to_all.10.block_ref = f32[8,24,512]{2,1,0:T(8,128)S(1)} all-to-all(f32[8,24,512]{2,1,0:T(8,128)S(1)} %outer.1), channel_id=1, replica_groups=mesh['tm'=8,'space'=4] {'tm'}, dimensions={0} | all-to-all | bytes 786432 | tf_op jit(solution)/shard_map/all_to_all | solution.py:385
  30.0 0.4 mix.1
  30.4 14.5 %all_to_all.11 = f32[8,16,512]{2,1,0:T(8,128)S(1)} all-to-all(f32[8,16,512]{2,1,0:T(8,128)S(1)} %mix.1), channel_id=1, replica_groups=mesh['tm'=8,'space'=4] {'tm'}, dimensions={0} | all-to-all | bytes 524288 | tf_op jit(solution)/shard_map/all_to_all | solution.py:394
  44.8 0.9 %copy.8 = f32[8,16,512]{2,0,1:T(8,128)} copy(f32[8,16,512]{2,1,0:T(8,128)S(1)} %all_to_all.11) | data formatting | bytes 524288 | tf_op jit(solution)/shard_map/reshape | solution.py:395
Async XLA Ops:
  1.3 2.4 %collective-permute-start.1 = (f32[8,4,16,128]{3,2,1,0:T(8,128)S(1)}, f32[8,4,16,128]{3,2,1,0:T(8,128)S(1)}, u32[]{:S(2)}, u32[]{:S(2)}) collective-permute-start(f32[8,4,16,128]{3,2,1,0:T(8,128)S(1)} %get-tuple-element.23), channel_id=1, source_target_pairs={{0,1},{2,3},{1,0},{3,2},{4,5},{6,7},{5,4},{7,6},{8,9},{10,11},{9,8... | collective-permute-start | bytes 786440 | tf_op jit(solution)/shard_map/ppermute | solution.py:347
  1.8 6.9 %collective-permute-start = (f32[8,4,16,128]{3,2,1,0:T(8,128)S(1)}, f32[8,4,16,128]{3,2,1,0:T(8,128)S(1)}, u32[]{:S(2)}, u32[]{:S(2)}) collective-permute-start(f32[8,4,16,128]{3,2,1,0:T(8,128)S(1)} %get-tuple-element.22), channel_id=1, source_target_pairs={{1,2},{2,1},{5,6},{6,5},{9,10},{10,9},{13,14},{14,13},{17,18},{18,... | collective-permute-start | bytes 786440 | tf_op jit(solution)/shard_map/ppermute | solution.py:347

commit v4 on v3

--- a/solution.py
+++ b/solution.py
@@ -77,7 +77,7 @@
     return high, low, key
 
 
-def prepare_kernel(w1_ref, bias_ref, w2_ref, corr_ref, w1_out, w2_out, w2_half, mix_out, *, strips, slots):
+def prepare_kernel(w1_ref, bias_ref, w2_ref, corr_ref, w1_out, w2_out, w2_half, mix_out, *, tm, strips, slots):
     fields = w1_ref.shape[2]
     channels = w1_ref.shape[3]
     time = corr_ref.shape[1]
@@ -90,31 +90,38 @@
     table = jnp.concatenate(
         [w1_ref[a, b] for a, b in taps] + [bias_ref[...], jnp.zeros((3, channels), F32)], axis=0
     )
-    w_high, w_low = split(table)
     bias_row = j == 36
-    over_rows = (((0,), (0,)), ((), ()))
+    chosen = [
+        jnp.concatenate([(code + 4 * out == codes) | (bias_row & (key == place)) for out in range(WIN_OUT)], axis=1)
+        for codes, place in ((high_code, 0), (low_code, 1))
+    ]
+    chosen = jnp.concatenate([jnp.where(c, 1.0, 0.0) for c in chosen], axis=0).astype(BF16)
+    parts = [p.astype(F32) for p in split(table)]
+    blocks = lax.dot_general(
+        jnp.concatenate(parts, axis=0).astype(BF16), chosen, (((0,), (0,)), ((), ())), preferred_element_type=F32
+    )
     for out in range(WIN_OUT):
-        pick_high = jnp.where((code + 4 * out == high_code) | (bias_row & (key == 0)), 1.0, 0.0).astype(BF16)
-        pick_low = jnp.where((code + 4 * out == low_code) | (bias_row & (key == 1)), 1.0, 0.0).astype(BF16)
-        block = lax.dot_general(w_high, pick_high, over_rows, preferred_element_type=F32)
-        block += lax.dot_general(w_low, pick_low, over_rows, preferred_element_type=F32)
-        w1_out[out * channels : (out + 1) * channels, :] = block.astype(BF16)
+        w1_out[out * channels : (out + 1) * channels, :] = blocks[:, out * KEYS : (out + 1) * KEYS].astype(BF16)
     keys = WIN_OUT * channels
     spread = jnp.where(iota((channels, keys), 1) % channels == iota((channels, keys), 0), 1.0, 0.0).astype(BF16)
     halves = split(jnp.concatenate([w2_ref[a, b] for a, b in taps], axis=0) * TENDENCY)
-    tables = [jnp.dot(h, spread, preferred_element_type=F32).astype(BF16) for h in halves]
+    tables = jnp.concatenate([jnp.dot(h, spread, preferred_element_type=F32).astype(BF16) for h in halves], axis=1)
+    mj = iota((72, 36), 0)
+    mj_tap = jnp.where(mj >= 48, 2, jnp.where(mj >= 24, 1, 0))
+    source = mj_tap * 4 + mj % 4
+    repeat = jnp.concatenate(
+        [jnp.where(iota((72, 36), 1) == tap_row * 12 + source, 1.0, 0.0) for tap_row in range(3)], axis=0
+    ).astype(BF16)
+    repeated = jnp.dot(repeat, tables, preferred_element_type=F32)
     m = iota((72, keys), 0)
     m_row = (m - jnp.where(m >= 48, 48, jnp.where(m >= 24, 24, 0))) // 4
     k_row = iota((72, keys), 1) // channels
-    mj = iota((72, 36), 0)
-    mj_tap = jnp.where(mj >= 48, 2, jnp.where(mj >= 24, 1, 0))
     full = []
-    for table in tables:
+    for part in range(2):
         total = jnp.zeros((72, keys), F32)
         for tap_row in range(3):
-            pick = jnp.where(iota((72, 36), 1) == tap_row * 12 + mj_tap * 4 + mj % 4, 1.0, 0.0).astype(BF16)
-            part = jnp.dot(pick, table, preferred_element_type=F32)
-            total = total + jnp.where(k_row == m_row - 2 + tap_row, part, 0.0)
+            block = repeated[72 * tap_row : 72 * (tap_row + 1), keys * part : keys * (part + 1)]
+            total = total + jnp.where(k_row == m_row - 2 + tap_row, block, 0.0)
         full.append(total)
     even, keep = chip_side(strips)
     outside = (
@@ -134,24 +141,19 @@
     ]
     w2_half[0:48, :] = jnp.concatenate([high, high], axis=1)
     w2_half[48:, :] = jnp.concatenate([low, jnp.zeros((48, short), BF16)], axis=1)
-    keys = mix_out.shape[1]
-    block = (slots + 2) * fields
-    key = iota((time, keys), 1)
-    sender = key // block
-    row = key - sender * block
-    slot = slots * sender + row // fields
-    valid = row < (slots + 1) * fields
-    pick = jnp.where((iota((time, keys), 0) == slot) & valid, 1.0, 0.0)
-    total = jnp.zeros(mix_out.shape, F32)
-    wide = (time * fields, time)
-    repeat = jnp.where(iota(wide, 0) // fields == iota(wide, 1), 1.0, 0.0)
-    to_field = iota(mix_out.shape, 0) % fields
-    from_field = iota(mix_out.shape, 1) % fields
+    main = tm * slots * fields
+    key = iota((time, main + tm * fields), 1)
+    slot = jnp.where(key < main, key // fields, (key - main) // fields * slots + slots)
+    met = slot == iota(key.shape, 0)
     for f in range(fields):
-        part = jnp.dot(corr_ref[f], pick, precision=EXACT, preferred_element_type=F32)
-        part = jnp.dot(repeat, part, precision=EXACT, preferred_element_type=F32)
-        total = jnp.where((to_field == f) & (from_field == f), part, total)
-    mix_out[...] = total
+        pick = jnp.where(met & (key % fields == f), 1.0, 0.0).astype(BF16)
+        first = corr_ref[f].astype(BF16)
+        rest = corr_ref[f] - first.astype(F32)
+        second = rest.astype(BF16)
+        third = (rest - second.astype(F32)).astype(BF16)
+        total = jnp.dot(first, pick, preferred_element_type=F32)
+        total += jnp.dot(second, pick, preferred_element_type=F32) + jnp.dot(third, pick, preferred_element_type=F32)
+        mix_out[f * time : (f + 1) * time, :] = total
 
 
 def moved(value, shift):
@@ -167,17 +169,16 @@
 def window_keys(groups, bias):
     cols = groups[0].shape[1]
     front_high, front_low, back_high, back_low = [], [], [], []
+    high, low = split(jnp.concatenate(groups[:2], axis=0))
+    if len(groups) == 3:
+        rounded = groups[2].astype(BF16).astype(F32)
+        both = jnp.concatenate([rounded, groups[2] - rounded], axis=0).astype(BF16)
     for tap in range(3):
-        value = moved(jnp.concatenate(groups[:2], axis=0), 1 - tap)
-        high, low = split(value)
-        front_high += [high, low]
-        front_low.append(high)
+        front_low.append(moved(high, 1 - tap))
+        front_high += [front_low[-1], moved(low, 1 - tap)]
         if len(groups) == 3:
-            value = moved(groups[2], 1 - tap)
-            high = value.astype(BF16).astype(F32)
-            both = jnp.concatenate([high, value - high], axis=0).astype(BF16)
-            back_high.append(both)
-            back_low.append(both)
+            back_high.append(moved(both, 1 - tap))
+    back_low = back_high
     first = jnp.full((16, cols), 1.0 if bias else 0.0, BF16)
     return jnp.concatenate([first] + front_high + front_low + back_high + back_low, axis=0)
 
@@ -213,13 +214,23 @@
     return jnp.concatenate([ref[index, p, 8 * g : 8 * g + 8, :] for p in range(pieces)], axis=1)
 
 
+def staggered(slots, one_slot, together):
+    waiting = [one_slot(slot) for slot in range(slots)]
+    running = []
+    while waiting or running:
+        starting = len(waiting) if together else 1
+        running = waiting[:starting] + running
+        waiting = waiting[starting:]
+        running = [r for r in running if next(r, True) is None]
+
+
 def inner_kernel(own_ref, core_got_ref, w1_ref, w2_ref, w2_half_ref, kept_ref, *, strips, slots):
     even, _ = chip_side(strips)
 
     def pick(if_even, if_odd):
         return jnp.where(even, if_even, if_odd)
 
-    for slot in range(slots):
+    def one_slot(slot):
         line, ends = [], []
         for index in (slot, slots + slot):
             own = [read_group(own_ref, index, g) for g in range(4)]
@@ -229,6 +240,7 @@
         first = hidden_pair(line[0][0:3], line[1][0:3], w1_ref)
         second = hidden_pair(line[0][2:5], line[1][2:5], w1_ref)
         last = hidden_pair(ends[0], ends[1], w1_ref)
+        yield
         moved_on = []
         for kind in range(2):
             a = spread_hidden(first[kind], w2_ref[0])
@@ -237,12 +249,14 @@
             added = [a[0] + pick(0.0, c[1]), a[1], a[2] + b[0], b[1], b[2] + pick(c[0], 0.0)]
             moved_on.append([x + y for x, y in zip(line[kind], added)])
         s, t = moved_on
+        yield
         outer = hidden_pair(
             [pick(a, b) for a, b in zip(s[2:5], s[0:3])], [pick(a, b) for a, b in zip(t[2:5], t[0:3])], w1_ref
         )
         middle = hidden_pair(
             [pick(a, b) for a, b in zip(s[1:3], s[2:4])], [pick(a, b) for a, b in zip(t[1:3], t[2:4])], w1_ref
         )
+        yield
         u = spread_hidden(outer[1], w2_ref[0])
         v = spread_hidden(middle[1], w2_half_ref[...])
         kept = [
@@ -257,12 +271,15 @@
         for g, value in enumerate(kept):
             kept_ref[slot, 8 * g : 8 * g + 8, :] = value
 
+    staggered(slots, one_slot, False)
+
 
 def outer_kernel(own_ref, chip_got_ref, kept_ref, w1_ref, w2_ref, send_ref, *, strips, slots, parts_across):
     even, keep = chip_side(strips)
     cols = kept_ref.shape[2]
     width = cols // parts_across
     fields, rows = 4, 8
+    packed = send_ref.shape[2] > width
 
     def pick(if_even, if_odd):
         return jnp.where(even, if_even, if_odd)
@@ -273,41 +290,85 @@
     def send(value, slot):
         for y in range(rows):
             for block in range(parts_across):
-                send_ref[y * parts_across + block, slot * fields : (slot + 1) * fields, :] = value[
-                    y * fields : (y + 1) * fields, block * width : (block + 1) * width
-                ]
+                part = value[y * fields : (y + 1) * fields, block * width : (block + 1) * width]
+                if slot < slots or not packed:
+                    send_ref[y * parts_across + block, slot * fields : (slot + 1) * fields, 0:width] = part
+                    continue
+                for q in range(slots):
+                    send_ref[y * parts_across + block, q * fields : (q + 1) * fields, width:] = part[
+                        :, q * width // slots : (q + 1) * width // slots
+                    ]
 
     def start(slot):
         return jnp.concatenate([read_group(own_ref, slots + slot, g) for g in range(4)], axis=0)
 
-    send(start(0), 0)
-    for slot in range(slots):
-        f_outer, f_middle, f_inner, s_near, t_near, s_next, t_next = [
-            kept_ref[slot, 8 * g : 8 * g + 8, :] for g in range(7)
-        ]
+    def one_slot(slot):
+        near = [kept_ref[slot, 8 * g : 8 * g + 8, :] for g in (3, 4)]
         frames = []
         for index in (slot, slots + slot):
             chip = [read_group(chip_got_ref, index, g) for g in range(2)]
             own = [read_group(own_ref, index, g) for g in (0, 3)]
             frames.append([pick(chip[0], own[1]), pick(chip[1], chip[0]), pick(own[0], chip[1])])
         pair = hidden_pair(frames[0], frames[1], w1_ref)
-        state, tangent = [], []
-        for kind, (near, result) in enumerate(((s_near, state), (t_near, tangent))):
+        yield
+        moved_on = []
+        for kind in range(2):
             w = spread_hidden(pair[kind], w2_ref[1])
-            result += [(frames[kind][1] + w[1]) * keep, near + pick(w[2], w[0])]
+            moved_on.append([(frames[kind][1] + w[1]) * keep, near[kind] + pick(w[2], w[0])])
+        state, tangent = moved_on
+        yield
+        f_outer, f_middle, f_inner, s_next, t_next = [kept_ref[slot, 8 * g : 8 * g + 8, :] for g in (0, 1, 2, 5, 6)]
         pair = hidden_pair(in_order(state + [s_next]), in_order(tangent + [t_next]), w1_ref)
+        yield
         x = spread_hidden(pair[1], w2_ref[2])
         ends = [tangent[1] + x[1], f_inner + pick(x[2], x[0]), f_middle, f_outer]
         final = jnp.concatenate(in_order(ends), axis=0)
         send(start(slot + 1) - final if slot < slots - 1 else -final, slot + 1)
-    send_ref[:, (slots + 1) * fields :, :] = jnp.zeros((rows * parts_across, fields, width), F32)
-
-
-def mix_kernel(mix_ref, block_ref, out_ref):
-    count, rows, width = block_ref.shape
-    keys = block_ref[...].reshape(count * rows, width)
+
+    send(start(0), 0)
+    staggered(slots, one_slot, True)
+    if not packed:
+        send_ref[:, (slots + 1) * fields :, :] = jnp.zeros((rows * parts_across, fields, width), F32)
+
+
+def mix_kernel(mix_ref, block_ref, out_ref, *, slots):
+    count, pieces, rows, _ = out_ref.shape
+    width = pieces * LANES
+    fields = rows // slots
+    time = count * slots
+    main = block_ref[:, 0:rows, 0:width].reshape(count * rows, width)
+    if block_ref.shape[2] > width:
+        last = [
+            jnp.concatenate([block_ref[d, q * fields : (q + 1) * fields, width:] for d in range(count)], axis=0)
+            for q in range(slots)
+        ]
+        last = jnp.concatenate(last, axis=1)
+    else:
+        last = jnp.concatenate([block_ref[d, rows : rows + fields, :] for d in range(count)], axis=0)
+    keys = jnp.concatenate([main, last], axis=0)
     out = jnp.dot(mix_ref[...], keys, precision=EXACT, preferred_element_type=F32)
-    out_ref[...] = out.reshape(out_ref.shape)
+    for d in range(count):
+        for f in range(fields):
+            start = f * time + d * slots
+            for p in range(pieces):
+                out_ref[d, p, f * slots : (f + 1) * slots, :] = out[start : start + slots, p * LANES : (p + 1) * LANES]
+
+
+def place_kernel(rows_ref, out_hbm, out_ref, sems):
+    slots, fields, rows, cols = out_ref.shape
+    pieces = cols // LANES
+    copies = []
+    for slot in range(slots):
+        for f in range(fields):
+            for p in range(pieces):
+                line = (p * fields + f) * slots + slot
+                out_ref[slot, f, :, p * LANES : (p + 1) * LANES] = rows_ref[
+                    pl.ds(line, rows, stride=pieces * fields * slots), :
+                ]
+        copies.append(pltpu.make_async_copy(out_ref.at[slot], out_hbm.at[slot], sems.at[slot]))
+        copies[-1].start()
+    for copy in copies:
+        copy.wait()
 
 
 def params():
@@ -349,14 +410,15 @@
     chip_got = swapped(chip, 1)
     core_got = swapped(core, 0)
 
-    block_rows = (slots + 2) * fields
+    packed = width // slots % LANES == 0
+    block = (slots * fields, width + width // slots) if packed else ((slots + 2) * fields, width)
     w1, w2, w2_half, mix = pl.pallas_call(
-        functools.partial(prepare_kernel, strips=strips, slots=slots),
+        functools.partial(prepare_kernel, tm=tm, strips=strips, slots=slots),
         out_shape=(
             jax.ShapeDtypeStruct((WIN_OUT * channels, KEYS), BF16),
             jax.ShapeDtypeStruct((3, 144, 2 * WIN_OUT * channels), BF16),
             jax.ShapeDtypeStruct((96, WIN_OUT * channels), BF16),
-            jax.ShapeDtypeStruct((time * fields, tm * block_rows), F32),
+            jax.ShapeDtypeStruct((fields * time, tm * (slots + 1) * fields), F32),
         ),
         in_specs=[VMEM] * 4,
         out_specs=(VMEM,) * 4,
@@ -375,7 +437,7 @@
 
     send = pl.pallas_call(
         functools.partial(outer_kernel, strips=strips, slots=slots, parts_across=parts_across),
-        out_shape=jax.ShapeDtypeStruct((tm, block_rows, width), F32),
+        out_shape=jax.ShapeDtypeStruct((tm, *block), F32),
         in_specs=[VMEM] * 5,
         out_specs=VMEM,
         compiler_params=params(),
@@ -384,16 +446,23 @@
 
     blocks = lax.all_to_all(send, "tm", split_axis=0, concat_axis=0, tiled=True)
     mixed = pl.pallas_call(
-        mix_kernel,
-        out_shape=jax.ShapeDtypeStruct((tm, slots * fields, width), F32),
+        functools.partial(mix_kernel, slots=slots),
+        out_shape=jax.ShapeDtypeStruct((tm, width // LANES, slots * fields, LANES), F32),
         in_specs=[VMEM] * 2,
         out_specs=VMEM,
         compiler_params=params(),
         name="mix",
     )(mix, blocks)
     back = lax.all_to_all(mixed, "tm", split_axis=0, concat_axis=0, tiled=True)
-    back = back.reshape(rows, parts_across, slots, fields, width)
-    return jnp.transpose(back, (2, 3, 0, 1, 4)).reshape(slots, fields, rows, cols)
+    return pl.pallas_call(
+        place_kernel,
+        out_shape=jax.ShapeDtypeStruct(increment.shape, F32),
+        in_specs=[VMEM],
+        out_specs=hbm,
+        scratch_shapes=[strip, pltpu.SemaphoreType.DMA((slots,))],
+        compiler_params=params(),
+        name="place",
+    )(back.reshape(-1, LANES))
 
 
 def solution(mesh):

time: 45.9 us -> 41.2 us (0.90)
  Pallas kernels: 11.5 us -> 8.7 us
  blocking collectives: 32.1 us -> 31 us
  local copies, waits for them, and re-layouts: 0.86 us -> 0 us
    pallas_call x1, Pallas kernels: 3.71 us -> 1.98 us  [body(): pl.pallas_call(functools.partial(outer_kernel, strips=strips, slots=slots...]
    pallas_call x1, Pallas kernels: 4.97 us -> 3.79 us  [body(): pl.pallas_call(functools.partial(inner_kernel, strips=strips, slots=slots...]
    reshape x1 -> x0, local copies, waits for them, and re-layouts: 0.86 us -> none  [body(): back = back.reshape(rows, parts_across, slots, fields, width)]
    all_to_all x1, blocking collectives: 17.6 us -> 16.9 us  [body(): blocks = lax.all_to_all(send, 'tm', split_axis=0, concat_axis=0, tiled=True)]
    pallas_call x2 -> x3, Pallas kernels: 1.6 us -> 1.69 us  [the longest x1 0.82 us: body(): pl.pallas_call(place_kernel, out_shape=jax.ShapeDtypeStruct(increment.sha...]
  transfers between devices with their start and end apart: 2 -> 2, of which waited for: 0 -> 0; matrix products, arithmetic and copies ran while one was open for 0% -> 0% of each run, Pallas kernels for 14% -> 10%
where the time goes in v4:
time: 41.2 us; the launch traced here: 41 us
  blocking collectives  31 us (75%)
  Pallas kernels  8.7 us (21%)
  starting transfers between devices  1.18 us (3%)
    all_to_all x1, blocking collectives, body(): blocks = lax.all_to_all(send, 'tm', split_axis=0, concat_axis=0, tiled=True)  16.9 us
    all_to_all x1, blocking collectives, body(): back = lax.all_to_all(mixed, 'tm', split_axis=0, concat_axis=0, tiled=True)  14.1 us
    pallas_call x1, Pallas kernels, body(): pl.pallas_call(functools.partial(inner_kernel, strips=strips, slots=slots...  3.79 us
    pallas_call x1, Pallas kernels, body(): pl.pallas_call(functools.partial(outer_kernel, strips=strips, slots=slots...  1.98 us
    pallas_call x1, Pallas kernels, body(): pl.pallas_call(pack_kernel, out_shape=(whole, half, half, *loaded), in_sp...  1.25 us
    ppermute x2, starting transfers between devices, swapped(): return lax.ppermute(value, 'space', pairs + [(j, i) for i, j in pairs])  1.18 us
  transfers between devices with their start and end apart: 2, of which 0 were waited for; matrix products, arithmetic and copies ran while one was open for 0% of the time, Pallas kernels for 10%

profile of v4, /device:TPU:0, one launch (start us, length us, event | category | flops | bytes accessed | tf_op | source)
XLA Modules:
  0.0 41.0 jit_solution(15313538573749124719)
XLA Ops:
  0.0 1.2 %pack.1 = (f32[8,4,32,128]{3,2,1,0:T(8,128)S(1)}, f32[8,4,16,128]{3,2,1,0:T(8,128)S(1)}, f32[8,4,16,128]{3,2,1,0:T(8,128)S(1)}, f32[3,3,4,32]{3,2,1,0:T(4,128)S(...) custom-call(f32[4,4,8,512]{3,2,1,0:T(8,128)} %traj_hbm.1, ...), custom_call_target="tpu_custom_call" | custom-call | tf_op jit(solution)/shard_map/pack/pallas_call | solution.py:396
  1.3 0.5 %collective-permute-start.1 = (f32[8,4,16,128]{3,2,1,0:T(8,128)S(1)}, f32[8,4,16,128]{3,2,1,0:T(8,128)S(1)}, u32[]{:S(2)}, u32[]{:S(2)}) collective-permute-start(f32[8,4,16,128]{3,2,1,0:T(8,128)S(1)} %get-tuple-element.23), channel_id=1, source_target_pairs={{0,1},{2,3},{1,0},{3,2},{4,5},{6,7},{5,4},{7,6},{8,9},{10,11},{9,8... | collective-permute-start | bytes 786440 | tf_op jit(solution)/shard_map/ppermute | solution.py:408
  1.8 0.7 %collective-permute-start = (f32[8,4,16,128]{3,2,1,0:T(8,128)S(1)}, f32[8,4,16,128]{3,2,1,0:T(8,128)S(1)}, u32[]{:S(2)}, u32[]{:S(2)}) collective-permute-start(f32[8,4,16,128]{3,2,1,0:T(8,128)S(1)} %get-tuple-element.22), channel_id=1, source_target_pairs={{1,2},{2,1},{5,6},{6,5},{9,10},{10,9},{13,14},{14,13},{17,18},{18,... | collective-permute-start | bytes 786440 | tf_op jit(solution)/shard_map/ppermute | solution.py:408
  2.4 0.5 %prepare.1 = (bf16[128,256]{1,0:T(8,128)(2,1)S(1)}, bf16[3,144,256]{2,1,0:T(8,128)(2,1)S(1)}, bf16[96,128]{1,0:T(8,128)(2,1)S(1)}, f32[128,160]{1,0:T(8,128)S(1)}) custom-call(f32[3,3,4,32]{3,2,1,0:T(4,128)S(1)} %get-tuple-element.16.w1_ref, f32[1,32]{1,0:T(1,128)S(1)} %get-tuple-element.17.bias_ref, f32[3,3,4,32]{3,2,1,0:T(4,128)S(1)} %get-tuple-element.18.w2_ref, ...), custom_call_target="tpu_custom_call" | custom-call | tf_op jit(solution)/shard_map/prepare/pallas_call | solution.py:415
  2.9 0.0 collective-permute-done.1.core_got_ref
  2.9 3.8 %inner.1.kept_ref = f32[4,56,512]{2,1,0:T(8,128)S(1)} custom-call(f32[8,4,32,128]{3,2,1,0:T(8,128)S(1)} %get-tuple-element.21.own_ref, f32[8,4,16,128]{3,2,1,0:T(8,128)S(1)} %collective-permute-done.1.core_got_ref, bf16[128,256]{1,0:T(8,128)(2,1)S(1)} %get-tuple-element.24.w1_ref, bf16[3,144,256]{2,1,0:T(8,128)(2,1)S(1)} %get-tuple-element.25.w2_ref, ...), custom_call_target="tpu_custom_call" | custom-call | tf_op jit(solution)/shard_map/inner/pallas_call | solution.py:429
  6.7 0.0 collective-permute-done.chip_got_ref
  6.7 2.0 %outer.1 = f32[8,16,640]{2,1,0:T(8,128)S(1)} custom-call(f32[8,4,32,128]{3,2,1,0:T(8,128)S(1)} %get-tuple-element.21.own_ref, f32[8,4,16,128]{3,2,1,0:T(8,128)S(1)} %collective-permute-done.chip_got_ref, f32[4,56,512]{2,1,0:T(8,128)S(1)} %inner.1.kept_ref, bf16[128,256]{1,0:T(8,128)(2,1)S(1)} %get-tuple-element.24.w1_ref, ...), custom_call_target="tpu_custom_call" | custom-call | tf_op jit(solution)/shard_map/outer/pallas_call | solution.py:438
  8.7 16.9 %all_to_all.10.block_ref = f32[8,16,640]{2,1,0:T(8,128)S(1)} all-to-all(f32[8,16,640]{2,1,0:T(8,128)S(1)} %outer.1), channel_id=1, replica_groups=mesh['tm'=8,'space'=4] {'tm'}, dimensions={0} | all-to-all | bytes 655360 | tf_op jit(solution)/shard_map/all_to_all | solution.py:447
  25.6 0.4 mix.1
  26.0 14.1 %all_to_all.11 = f32[8,4,16,128]{3,2,1,0:T(8,128)S(1)} all-to-all(f32[8,4,16,128]{3,2,1,0:T(8,128)S(1)} %mix.1), channel_id=1, replica_groups=mesh['tm'=8,'space'=4] {'tm'}, dimensions={0} | all-to-all | bytes 524288 | tf_op jit(solution)/shard_map/all_to_all | solution.py:456
  40.1 0.8 %place.1 = f32[4,4,8,512]{3,2,1,0:T(8,128)} custom-call(f32[512,128]{1,0:T(8,128)S(1)} %bitcast.4), custom_call_target="tpu_custom_call" | custom-call | tf_op jit(solution)/shard_map/place/pallas_call | solution.py:457
Async XLA Ops:
  1.3 1.7 %collective-permute-start.1 = (f32[8,4,16,128]{3,2,1,0:T(8,128)S(1)}, f32[8,4,16,128]{3,2,1,0:T(8,128)S(1)}, u32[]{:S(2)}, u32[]{:S(2)}) collective-permute-start(f32[8,4,16,128]{3,2,1,0:T(8,128)S(1)} %get-tuple-element.23), channel_id=1, source_target_pairs={{0,1},{2,3},{1,0},{3,2},{4,5},{6,7},{5,4},{7,6},{8,9},{10,11},{9,8... | collective-permute-start | bytes 786440 | tf_op jit(solution)/shard_map/ppermute | solution.py:408
  1.8 5.0 %collective-permute-start = (f32[8,4,16,128]{3,2,1,0:T(8,128)S(1)}, f32[8,4,16,128]{3,2,1,0:T(8,128)S(1)}, u32[]{:S(2)}, u32[]{:S(2)}) collective-permute-start(f32[8,4,16,128]{3,2,1,0:T(8,128)S(1)} %get-tuple-element.22), channel_id=1, source_target_pairs={{1,2},{2,1},{5,6},{6,5},{9,10},{10,9},{13,14},{14,13},{17,18},{18,... | collective-permute-start | bytes 786440 | tf_op jit(solution)/shard_map/ppermute | solution.py:408

commit v5 on v4

--- a/solution.py
+++ b/solution.py
@@ -423,6 +423,7 @@
         in_specs=[VMEM] * 4,
         out_specs=(VMEM,) * 4,
         compiler_params=params(),
+        cost_estimate=pl.CostEstimate(flops=10**12, bytes_accessed=10**9, transcendentals=0),
         name="prepare",
     )(w1_taps, bias_row, w2_taps, correlation)
 

time: 41.2 us -> 46.5 us (1.13)
  starting transfers between devices: 1.18 us -> 5.06 us
  Pallas kernels: 8.7 us -> 11.4 us
  blocking collectives: 31 us -> 28.7 us
  waiting for transfers between devices: 0.01 us -> 1.04 us
    ppermute x2, starting transfers between devices: 1.18 us -> 5.06 us  [swapped(): return lax.ppermute(value, 'space', pairs + [(j, i) for i, j in pairs])]
    all_to_all x1, blocking collectives: 14.1 us -> 11.6 us  [body(): back = lax.all_to_all(mixed, 'tm', split_axis=0, concat_axis=0, tiled=True)]
    ppermute x2, waiting for transfers between devices: 0.01 us -> 1.04 us  [swapped(): return lax.ppermute(value, 'space', pairs + [(j, i) for i, j in pairs])]
    pallas_call x1, Pallas kernels: 1.98 us -> 2.93 us  [body(): pl.pallas_call(functools.partial(outer_kernel, strips=strips, slots=slots...]
    pallas_call x1, Pallas kernels: 3.79 us -> 4.72 us  [body(): pl.pallas_call(functools.partial(inner_kernel, strips=strips, slots=slots...]
    pallas_call x1, Pallas kernels: 1.25 us -> 2.02 us  [body(): pl.pallas_call(pack_kernel, out_shape=(whole, half, half, *loaded), in_sp...]
  transfers between devices with their start and end apart: 2 -> 2, of which waited for: 0 -> 1; matrix products, arithmetic and copies ran while one was open for 0% -> 0% of each run, Pallas kernels for 10% -> 11%
where the time goes in v5:
time: 46.5 us; the launch traced here: 46.2 us
  blocking collectives  28.7 us (62%)
  Pallas kernels  11.4 us (25%)
  starting transfers between devices  5.06 us (11%)
  waiting for transfers between devices  1.04 us (2%)
    all_to_all x1, blocking collectives, body(): blocks = lax.all_to_all(send, 'tm', split_axis=0, concat_axis=0, tiled=True)  17.1 us
    all_to_all x1, blocking collectives, body(): back = lax.all_to_all(mixed, 'tm', split_axis=0, concat_axis=0, tiled=True)  11.6 us
    ppermute x2, starting transfers between devices, swapped(): return lax.ppermute(value, 'space', pairs + [(j, i) for i, j in pairs])  5.06 us
    pallas_call x1, Pallas kernels, body(): pl.pallas_call(functools.partial(inner_kernel, strips=strips, slots=slots...  4.72 us
    pallas_call x1, Pallas kernels, body(): pl.pallas_call(functools.partial(outer_kernel, strips=strips, slots=slots...  2.93 us
    pallas_call x1, Pallas kernels, body(): pl.pallas_call(pack_kernel, out_shape=(whole, half, half, *loaded), in_sp...  2.02 us
    ppermute x2, waiting for transfers between devices, swapped(): return lax.ppermute(value, 'space', pairs + [(j, i) for i, j in pairs])  1.04 us
  transfers between devices with their start and end apart: 2, of which 1 were waited for; matrix products, arithmetic and copies ran while one was open for 0% of the time, Pallas kernels for 11%

profile of v5, /device:TPU:0, one launch (start us, length us, event | category | flops | bytes accessed | tf_op | source)
XLA Modules:
  0.0 46.2 jit_solution(11929682254727835899)
XLA Ops:
  0.0 2.0 %pack.1 = (f32[8,4,32,128]{3,2,1,0:T(8,128)S(1)}, f32[8,4,16,128]{3,2,1,0:T(8,128)}, f32[8,4,16,128]{3,2,1,0:T(8,128)}, f32[3,3,4,32]{3,2,1,0:T(4,128)S(1)}, f32...) custom-call(f32[4,4,8,512]{3,2,1,0:T(8,128)} %traj_hbm.1, f32[4,4,8,512]{3,2,1,0:T(8,128)} %incr_hbm.1, ...), custom_call_target="tpu_custom_call" | custom-call | tf_op jit(solution)/shard_map/pack/pallas_call | solution.py:396
  2.0 1.4 %collective-permute-start = (f32[8,4,16,128]{3,2,1,0:T(8,128)}, f32[8,4,16,128]{3,2,1,0:T(8,128)}, u32[]{:S(2)}, u32[]{:S(2)}) collective-permute-start(f32[8,4,16,128]{3,2,1,0:T(8,128)} %get-tuple-element.22), channel_id=1, source_target_pairs={{1,2},{2,1},{5,6},{6,5},{9,10},{10,9},{13,14},{14,13},{17,18},{18,... | collective-permute-start | bytes 786440 | tf_op jit(solution)/shard_map/ppermute | solution.py:408
  3.4 3.7 %collective-permute-start.1 = (f32[8,4,16,128]{3,2,1,0:T(8,128)}, f32[8,4,16,128]{3,2,1,0:T(8,128)}, u32[]{:S(2)}, u32[]{:S(2)}) collective-permute-start(f32[8,4,16,128]{3,2,1,0:T(8,128)} %get-tuple-element.23), channel_id=1, source_target_pairs={{0,1},{2,3},{1,0},{3,2},{4,5},{6,7},{5,4},{7,6},{8,9},{10,11},{9,8... | collective-permute-start | bytes 786440 | tf_op jit(solution)/shard_map/ppermute | solution.py:408
  7.1 0.5 %prepare.1 = (bf16[128,256]{1,0:T(8,128)(2,1)S(1)}, bf16[3,144,256]{2,1,0:T(8,128)(2,1)S(1)}, bf16[96,128]{1,0:T(8,128)(2,1)S(1)}, f32[128,160]{1,0:T(8,128)S(1)}) custom-call(f32[3,3,4,32]{3,2,1,0:T(4,128)S(1)} %get-tuple-element.16.w1_ref, f32[1,32]{1,0:T(1,128)S(1)} %get-tuple-element.17.bias_ref, f32[3,3,4,32]{3,2,1,0:T(4,128)S(1)} %get-tuple-element.18.w2_ref, ...), custom_call_target="tpu_custom_call" | custom-call | flops 999999995904 | bytes 1000000000 | tf_op jit(solution)/shard_map/prepare/pallas_call | solution.py:415
  7.6 1.0 %collective-permute-done.1.core_got_ref = f32[8,4,16,128]{3,2,1,0:T(8,128)} collective-permute-done((f32[8,4,16,128]{3,2,1,0:T(8,128)}, f32[8,4,16,128]{3,2,1,0:T(8,128)}, u32[]{:S(2)}, u32[]{:S(2)}) %collective-permute-start.1) | collective-permute-done | bytes 262176 | tf_op jit(solution)/shard_map/ppermute | solution.py:408
  8.6 4.7 %inner.1.kept_ref = f32[4,56,512]{2,1,0:T(8,128)S(1)} custom-call(f32[8,4,32,128]{3,2,1,0:T(8,128)S(1)} %get-tuple-element.21.own_ref, f32[8,4,16,128]{3,2,1,0:T(8,128)} %collective-permute-done.1.core_got_ref, bf16[128,256]{1,0:T(8,128)(2,1)S(1)} %get-tuple-element.24.w1_ref, bf16[3,144,256]{2,1,0:T(8,128)(2,1)S(1)} %get-tuple-element.25.w2_ref, ...), custom_call_target="tpu_custom_call" | custom-call | tf_op jit(solution)/shard_map/inner/pallas_call | solution.py:430
  13.3 0.0 collective-permute-done.chip_got_ref
  13.3 2.9 %outer.1 = f32[8,16,640]{2,1,0:T(8,128)S(1)} custom-call(f32[8,4,32,128]{3,2,1,0:T(8,128)S(1)} %get-tuple-element.21.own_ref, f32[8,4,16,128]{3,2,1,0:T(8,128)} %collective-permute-done.chip_got_ref, f32[4,56,512]{2,1,0:T(8,128)S(1)} %inner.1.kept_ref, bf16[128,256]{1,0:T(8,128)(2,1)S(1)} %get-tuple-element.24.w1_ref, ...), custom_call_target="tpu_custom_call" | custom-call | tf_op jit(solution)/shard_map/outer/pallas_call | solution.py:439
  16.3 17.1 %all_to_all.10.block_ref = f32[8,16,640]{2,1,0:T(8,128)S(1)} all-to-all(f32[8,16,640]{2,1,0:T(8,128)S(1)} %outer.1), channel_id=1, replica_groups=mesh['tm'=8,'space'=4] {'tm'}, dimensions={0} | all-to-all | bytes 655360 | tf_op jit(solution)/shard_map/all_to_all | solution.py:448
  33.4 0.4 mix.1
  33.8 11.6 %all_to_all.11 = f32[8,4,16,128]{3,2,1,0:T(8,128)S(1)} all-to-all(f32[8,4,16,128]{3,2,1,0:T(8,128)S(1)} %mix.1), channel_id=1, replica_groups=mesh['tm'=8,'space'=4] {'tm'}, dimensions={0} | all-to-all | bytes 524288 | tf_op jit(solution)/shard_map/all_to_all | solution.py:457
  45.4 0.8 %place.1 = f32[4,4,8,512]{3,2,1,0:T(8,128)} custom-call(f32[512,128]{1,0:T(8,128)S(1)} %bitcast.4), custom_call_target="tpu_custom_call" | custom-call | tf_op jit(solution)/shard_map/place/pallas_call | solution.py:458
Async XLA Ops:
  2.0 11.3 %collective-permute-start = (f32[8,4,16,128]{3,2,1,0:T(8,128)}, f32[8,4,16,128]{3,2,1,0:T(8,128)}, u32[]{:S(2)}, u32[]{:S(2)}) collective-permute-start(f32[8,4,16,128]{3,2,1,0:T(8,128)} %get-tuple-element.22), channel_id=1, source_target_pairs={{1,2},{2,1},{5,6},{6,5},{9,10},{10,9},{13,14},{14,13},{17,18},{18,... | collective-permute-start | bytes 786440 | tf_op jit(solution)/shard_map/ppermute | solution.py:408
  3.4 5.2 %collective-permute-start.1 = (f32[8,4,16,128]{3,2,1,0:T(8,128)}, f32[8,4,16,128]{3,2,1,0:T(8,128)}, u32[]{:S(2)}, u32[]{:S(2)}) collective-permute-start(f32[8,4,16,128]{3,2,1,0:T(8,128)} %get-tuple-element.23), channel_id=1, source_target_pairs={{0,1},{2,3},{1,0},{3,2},{4,5},{6,7},{5,4},{7,6},{8,9},{10,11},{9,8... | collective-permute-start | bytes 786440 | tf_op jit(solution)/shard_map/ppermute | solution.py:408

commit v6 on v4

--- a/solution.py
+++ b/solution.py
@@ -19,6 +19,8 @@
 LANES = 128
 KEYS = 256
 HALF_KEYS = 160
+COLUMN_BLOCKS = 2
+CHUNK = 16
 
 
 def iota(shape, dim):
@@ -150,10 +152,9 @@
         first = corr_ref[f].astype(BF16)
         rest = corr_ref[f] - first.astype(F32)
         second = rest.astype(BF16)
-        third = (rest - second.astype(F32)).astype(BF16)
-        total = jnp.dot(first, pick, preferred_element_type=F32)
-        total += jnp.dot(second, pick, preferred_element_type=F32) + jnp.dot(third, pick, preferred_element_type=F32)
-        mix_out[f * time : (f + 1) * time, :] = total
+        rows = slice(f * time, (f + 1) * time)
+        high = jnp.dot(first, pick, preferred_element_type=F32).astype(BF16)
+        mix_out[rows, :] = jnp.concatenate([high, high, jnp.dot(second, pick, preferred_element_type=F32).astype(BF16)], axis=1)
 
 
 def moved(value, shift):
@@ -188,17 +189,33 @@
     if len(state_groups) == 2:
         rows, keys = rows // 2, HALF_KEYS
     w1 = w1_ref[0:rows, 0:keys]
-    z = jnp.dot(w1, window_keys(state_groups, True), preferred_element_type=F32)
-    dz = jnp.dot(w1, window_keys(tangent_groups, False), preferred_element_type=F32)
-    h = jnp.tanh(z)
-    return h, (1.0 - h * h) * dz
+    state_keys = window_keys(state_groups, True)
+    tangent_keys = window_keys(tangent_groups, False)
+    cols = state_keys.shape[1]
+    width = cols // COLUMN_BLOCKS
+    result = ([], [])
+    for start in range(0, cols, width):
+        z = jnp.dot(w1, state_keys[:, start : start + width], preferred_element_type=F32)
+        dz = jnp.dot(w1, tangent_keys[:, start : start + width], preferred_element_type=F32)
+        parts = ([], [], [], [])
+        for row in range(0, rows, CHUNK):
+            h = jnp.tanh(z[row : row + CHUNK])
+            g = (1.0 - h * h) * dz[row : row + CHUNK]
+            for place, part in zip(parts, (*split(h), *split(g))):
+                place.append(part)
+        result[0].append(jnp.concatenate(parts[0] + parts[1], axis=0))
+        result[1].append(jnp.concatenate(parts[2] + parts[3], axis=0))
+    return result
 
 
 def spread_hidden(hidden, weight):
-    taps = jnp.dot(weight, jnp.concatenate(split(hidden), axis=0), preferred_element_type=F32)
-    half = taps.shape[0] // 2
-    taps = taps[:half] + taps[half:]
-    third = half // 3
+    taps = []
+    for block in hidden:
+        product = jnp.dot(weight, block, preferred_element_type=F32)
+        half = product.shape[0] // 2
+        taps.append(product[:half] + product[half:])
+    taps = jnp.concatenate(taps, axis=1)
+    third = taps.shape[0] // 3
     total = moved(taps[0:third], 1) + taps[third : 2 * third] + moved(taps[2 * third :], -1)
     return [total[g : g + 8] for g in range(0, third, 8)]
 
@@ -346,7 +363,8 @@
     else:
         last = jnp.concatenate([block_ref[d, rows : rows + fields, :] for d in range(count)], axis=0)
     keys = jnp.concatenate([main, last], axis=0)
-    out = jnp.dot(mix_ref[...], keys, precision=EXACT, preferred_element_type=F32)
+    high, low = split(keys)
+    out = jnp.dot(mix_ref[...], jnp.concatenate([high, low, high], axis=0), preferred_element_type=F32)
     for d in range(count):
         for f in range(fields):
             start = f * time + d * slots
@@ -418,7 +436,7 @@
             jax.ShapeDtypeStruct((WIN_OUT * channels, KEYS), BF16),
             jax.ShapeDtypeStruct((3, 144, 2 * WIN_OUT * channels), BF16),
             jax.ShapeDtypeStruct((96, WIN_OUT * channels), BF16),
-            jax.ShapeDtypeStruct((fields * time, tm * (slots + 1) * fields), F32),
+            jax.ShapeDtypeStruct((fields * time, 3 * tm * (slots + 1) * fields), BF16),
         ),
         in_specs=[VMEM] * 4,
         out_specs=(VMEM,) * 4,

time: 41.2 us -> 40.7 us (0.988)
  Pallas kernels: 8.7 us -> 8.22 us
where the time goes in v6:
time: 40.7 us; the launch traced here: 40.5 us
  blocking collectives  31 us (76%)
  Pallas kernels  8.22 us (20%)
  starting transfers between devices  1.18 us (3%)
    all_to_all x1, blocking collectives, body(): blocks = lax.all_to_all(send, 'tm', split_axis=0, concat_axis=0, tiled=True)  16.7 us
    all_to_all x1, blocking collectives, body(): back = lax.all_to_all(mixed, 'tm', split_axis=0, concat_axis=0, tiled=True)  14.3 us
    pallas_call x1, Pallas kernels, body(): pl.pallas_call(functools.partial(inner_kernel, strips=strips, slots=slots...  3.64 us
    pallas_call x1, Pallas kernels, body(): pl.pallas_call(functools.partial(outer_kernel, strips=strips, slots=slots...  1.8 us
    pallas_call x1, Pallas kernels, body(): pl.pallas_call(pack_kernel, out_shape=(whole, half, half, *loaded), in_sp...  1.25 us
    ppermute x2, starting transfers between devices, swapped(): return lax.ppermute(value, 'space', pairs + [(j, i) for i, j in pairs])  1.18 us
    pallas_call x1, Pallas kernels, body(): pl.pallas_call(place_kernel, out_shape=jax.ShapeDtypeStruct(increment.sha...  0.82 us
  transfers between devices with their start and end apart: 2, of which 0 were waited for; matrix products, arithmetic and copies ran while one was open for 0% of the time, Pallas kernels for 10%

profile of v6, /device:TPU:0, one launch (start us, length us, event | category | flops | bytes accessed | tf_op | source)
XLA Modules:
  0.0 40.5 jit_solution(7775743930174619536)
XLA Ops:
  0.0 1.2 %pack.1 = (f32[8,4,32,128]{3,2,1,0:T(8,128)S(1)}, f32[8,4,16,128]{3,2,1,0:T(8,128)S(1)}, f32[8,4,16,128]{3,2,1,0:T(8,128)S(1)}, f32[3,3,4,32]{3,2,1,0:T(4,128)S(...) custom-call(f32[4,4,8,512]{3,2,1,0:T(8,128)} %traj_hbm.1, ...), custom_call_target="tpu_custom_call" | custom-call | tf_op jit(solution)/shard_map/pack/pallas_call | solution.py:414
  1.3 0.5 %collective-permute-start.1 = (f32[8,4,16,128]{3,2,1,0:T(8,128)S(1)}, f32[8,4,16,128]{3,2,1,0:T(8,128)S(1)}, u32[]{:S(2)}, u32[]{:S(2)}) collective-permute-start(f32[8,4,16,128]{3,2,1,0:T(8,128)S(1)} %get-tuple-element.23), channel_id=1, source_target_pairs={{0,1},{2,3},{1,0},{3,2},{4,5},{6,7},{5,4},{7,6},{8,9},{10,11},{9,8... | collective-permute-start | bytes 786440 | tf_op jit(solution)/shard_map/ppermute | solution.py:426
  1.8 0.7 %collective-permute-start = (f32[8,4,16,128]{3,2,1,0:T(8,128)S(1)}, f32[8,4,16,128]{3,2,1,0:T(8,128)S(1)}, u32[]{:S(2)}, u32[]{:S(2)}) collective-permute-start(f32[8,4,16,128]{3,2,1,0:T(8,128)S(1)} %get-tuple-element.22), channel_id=1, source_target_pairs={{1,2},{2,1},{5,6},{6,5},{9,10},{10,9},{13,14},{14,13},{17,18},{18,... | collective-permute-start | bytes 786440 | tf_op jit(solution)/shard_map/ppermute | solution.py:426
  2.4 0.5 %prepare.1 = (bf16[128,256]{1,0:T(8,128)(2,1)S(1)}, bf16[3,144,256]{2,1,0:T(8,128)(2,1)S(1)}, bf16[96,128]{1,0:T(8,128)(2,1)S(1)}, bf16[128,480]{1,0:T(8,128)(2,1)S(1)}) custom-call(f32[3,3,4,32]{3,2,1,0:T(4,128)S(1)} %get-tuple-element.16.w1_ref, f32[1,32]{1,0:T(1,128)S(1)} %get-tuple-element.17.bias_ref, f32[3,3,4,32]{3,2,1,0:T(4,128)S(1)} %get-tuple-element.18.w2_ref, ...), custom_call_target="tpu_custom_call" | custom-call | tf_op jit(solution)/shard_map/prepare/pallas_call | solution.py:433
  2.9 0.0 collective-permute-done.1.core_got_ref
  2.9 3.6 %inner.1.kept_ref = f32[4,56,512]{2,1,0:T(8,128)S(1)} custom-call(f32[8,4,32,128]{3,2,1,0:T(8,128)S(1)} %get-tuple-element.21.own_ref, f32[8,4,16,128]{3,2,1,0:T(8,128)S(1)} %collective-permute-done.1.core_got_ref, bf16[128,256]{1,0:T(8,128)(2,1)S(1)} %get-tuple-element.24.w1_ref, bf16[3,144,256]{2,1,0:T(8,128)(2,1)S(1)} %get-tuple-element.25.w2_ref, ...), custom_call_target="tpu_custom_call" | custom-call | tf_op jit(solution)/shard_map/inner/pallas_call | solution.py:447
  6.6 0.0 collective-permute-done.chip_got_ref
  6.6 1.8 %outer.1 = f32[8,16,640]{2,1,0:T(8,128)S(1)} custom-call(f32[8,4,32,128]{3,2,1,0:T(8,128)S(1)} %get-tuple-element.21.own_ref, f32[8,4,16,128]{3,2,1,0:T(8,128)S(1)} %collective-permute-done.chip_got_ref, f32[4,56,512]{2,1,0:T(8,128)S(1)} %inner.1.kept_ref, bf16[128,256]{1,0:T(8,128)(2,1)S(1)} %get-tuple-element.24.w1_ref, ...), custom_call_target="tpu_custom_call" | custom-call | tf_op jit(solution)/shard_map/outer/pallas_call | solution.py:456
  8.4 16.7 %all_to_all.10.block_ref = f32[8,16,640]{2,1,0:T(8,128)S(1)} all-to-all(f32[8,16,640]{2,1,0:T(8,128)S(1)} %outer.1), channel_id=1, replica_groups=mesh['tm'=8,'space'=4] {'tm'}, dimensions={0} | all-to-all | bytes 655360 | tf_op jit(solution)/shard_map/all_to_all | solution.py:465
  25.1 0.2 mix.1
  25.4 14.3 %all_to_all.11 = f32[8,4,16,128]{3,2,1,0:T(8,128)S(1)} all-to-all(f32[8,4,16,128]{3,2,1,0:T(8,128)S(1)} %mix.1), channel_id=1, replica_groups=mesh['tm'=8,'space'=4] {'tm'}, dimensions={0} | all-to-all | bytes 524288 | tf_op jit(solution)/shard_map/all_to_all | solution.py:474
  39.6 0.8 %place.1 = f32[4,4,8,512]{3,2,1,0:T(8,128)} custom-call(f32[512,128]{1,0:T(8,128)S(1)} %bitcast.4), custom_call_target="tpu_custom_call" | custom-call | tf_op jit(solution)/shard_map/place/pallas_call | solution.py:475
Async XLA Ops:
  1.3 1.7 %collective-permute-start.1 = (f32[8,4,16,128]{3,2,1,0:T(8,128)S(1)}, f32[8,4,16,128]{3,2,1,0:T(8,128)S(1)}, u32[]{:S(2)}, u32[]{:S(2)}) collective-permute-start(f32[8,4,16,128]{3,2,1,0:T(8,128)S(1)} %get-tuple-element.23), channel_id=1, source_target_pairs={{0,1},{2,3},{1,0},{3,2},{4,5},{6,7},{5,4},{7,6},{8,9},{10,11},{9,8... | collective-permute-start | bytes 786440 | tf_op jit(solution)/shard_map/ppermute | solution.py:426
  1.8 4.8 %collective-permute-start = (f32[8,4,16,128]{3,2,1,0:T(8,128)S(1)}, f32[8,4,16,128]{3,2,1,0:T(8,128)S(1)}, u32[]{:S(2)}, u32[]{:S(2)}) collective-permute-start(f32[8,4,16,128]{3,2,1,0:T(8,128)S(1)} %get-tuple-element.22), channel_id=1, source_target_pairs={{1,2},{2,1},{5,6},{6,5},{9,10},{10,9},{13,14},{14,13},{17,18},{18,... | collective-permute-start | bytes 786440 | tf_op jit(solution)/shard_map/ppermute | solution.py:426

commit v7 on v6

--- a/solution.py
+++ b/solution.py
@@ -79,7 +79,7 @@
     return high, low, key
 
 
-def prepare_kernel(w1_ref, bias_ref, w2_ref, corr_ref, w1_out, w2_out, w2_half, mix_out, *, tm, strips, slots):
+def prepare_kernel(w1_ref, bias_ref, w2_ref, corr_ref, w1_out, w2_out, w2_side, w2_half, w2_end, mix_out, *, tm, strips, slots):
     fields = w1_ref.shape[2]
     channels = w1_ref.shape[3]
     time = corr_ref.shape[1]
@@ -126,23 +126,32 @@
             total = total + jnp.where(k_row == m_row - 2 + tap_row, block, 0.0)
         full.append(total)
     even, keep = chip_side(strips)
-    outside = (
-        None,
-        (even & (k_row < 3)) | (~even & (k_row > 0)),
-        (even & (k_row < 1)) | (~even & (k_row > 2)),
-    )
-    for form, rows_out in enumerate(outside):
-        high, low = [t if rows_out is None else jnp.where(rows_out, t * keep, t) for t in full]
-        w2_out[form, 0:72, 0:keys] = high.astype(BF16)
-        w2_out[form, 0:72, keys:] = high.astype(BF16)
-        w2_out[form, 72:, 0:keys] = low.astype(BF16)
-        w2_out[form, 72:, keys:] = jnp.zeros((72, keys), BF16)
+
+    def operand(tables):
+        high, low = tables
+        return jnp.concatenate(
+            [jnp.concatenate([high, high], axis=1), jnp.concatenate([low, jnp.zeros(low.shape, F32)], axis=1)], axis=0
+        ).astype(BF16)
+
+    def groups_of(table, if_even, if_odd, count, width):
+        rows = [
+            jnp.where(even, table[24 * t + 8 * e : 24 * t + 8 * e + 8], table[24 * t + 8 * o : 24 * t + 8 * o + 8])
+            for t in range(3)
+            for e, o in list(zip(if_even, if_odd))[:count]
+        ]
+        return jnp.concatenate(rows, axis=0)[:, 0:width]
+
+    first_out = (even & (k_row < 3)) | (~even & (k_row > 0))
+    second_out = (even & (k_row < 1)) | (~even & (k_row > 2))
+    w2_out[...] = operand(full)
+    for form, (rows_out, if_even, if_odd) in enumerate(
+        ((first_out, (1, 2), (1, 0)), (second_out, (1, 2), (1, 0)), (None, (1, 0), (1, 2)))
+    ):
+        kept = [t if rows_out is None else jnp.where(rows_out, t * keep, t) for t in full]
+        w2_side[form] = operand([groups_of(t, if_even, if_odd, 2, keys) for t in kept])
     short = keys // 2
-    high, low = [
-        jnp.concatenate([t[24 * tap : 24 * tap + 16, 0:short] for tap in range(3)], axis=0).astype(BF16) for t in full
-    ]
-    w2_half[0:48, :] = jnp.concatenate([high, high], axis=1)
-    w2_half[48:, :] = jnp.concatenate([low, jnp.zeros((48, short), BF16)], axis=1)
+    w2_half[...] = operand([groups_of(t, (0, 1), (0, 1), 2, short) for t in full])
+    w2_end[...] = operand([groups_of(t, (0,), (1,), 1, short) for t in full])
     main = tm * slots * fields
     key = iota((time, main + tm * fields), 1)
     slot = jnp.where(key < main, key // fields, (key - main) // fields * slots + slots)
@@ -241,7 +250,7 @@
         running = [r for r in running if next(r, True) is None]
 
 
-def inner_kernel(own_ref, core_got_ref, w1_ref, w2_ref, w2_half_ref, kept_ref, *, strips, slots):
+def inner_kernel(own_ref, core_got_ref, w1_ref, w2_ref, w2_side_ref, w2_half_ref, w2_end_ref, kept_ref, *, strips, slots):
     even, _ = chip_side(strips)
 
     def pick(if_even, if_odd):
@@ -260,10 +269,10 @@
         yield
         moved_on = []
         for kind in range(2):
-            a = spread_hidden(first[kind], w2_ref[0])
-            b = spread_hidden(second[kind], w2_ref[0])
-            c = spread_hidden(last[kind], w2_half_ref[...])
-            added = [a[0] + pick(0.0, c[1]), a[1], a[2] + b[0], b[1], b[2] + pick(c[0], 0.0)]
+            a = spread_hidden(first[kind], w2_ref[...])
+            b = spread_hidden(second[kind], w2_ref[...])
+            (c,) = spread_hidden(last[kind], w2_end_ref[...])
+            added = [a[0] + pick(0.0, c), a[1], a[2] + b[0], b[1], b[2] + pick(c, 0.0)]
             moved_on.append([x + y for x, y in zip(line[kind], added)])
         s, t = moved_on
         yield
@@ -274,11 +283,11 @@
             [pick(a, b) for a, b in zip(s[1:3], s[2:4])], [pick(a, b) for a, b in zip(t[1:3], t[2:4])], w1_ref
         )
         yield
-        u = spread_hidden(outer[1], w2_ref[0])
+        u = spread_hidden(outer[1], w2_side_ref[2])
         v = spread_hidden(middle[1], w2_half_ref[...])
         kept = [
-            pick(t[3], t[1]) + u[1],
-            t[2] + pick(u[0], u[2]) + pick(v[1], v[0]),
+            pick(t[3], t[1]) + u[0],
+            t[2] + u[1] + pick(v[1], v[0]),
             pick(t[1], t[3]) + pick(v[0], v[1]),
             pick(s[0], s[4]),
             pick(t[0], t[4]),
@@ -291,7 +300,7 @@
     staggered(slots, one_slot, False)
 
 
-def outer_kernel(own_ref, chip_got_ref, kept_ref, w1_ref, w2_ref, send_ref, *, strips, slots, parts_across):
+def outer_kernel(own_ref, chip_got_ref, kept_ref, w1_ref, w2_side_ref, send_ref, *, strips, slots, parts_across):
     even, keep = chip_side(strips)
     cols = kept_ref.shape[2]
     width = cols // parts_across
@@ -330,15 +339,15 @@
         yield
         moved_on = []
         for kind in range(2):
-            w = spread_hidden(pair[kind], w2_ref[1])
-            moved_on.append([(frames[kind][1] + w[1]) * keep, near[kind] + pick(w[2], w[0])])
+            w = spread_hidden(pair[kind], w2_side_ref[0])
+            moved_on.append([(frames[kind][1] + w[0]) * keep, near[kind] + w[1]])
         state, tangent = moved_on
         yield
         f_outer, f_middle, f_inner, s_next, t_next = [kept_ref[slot, 8 * g : 8 * g + 8, :] for g in (0, 1, 2, 5, 6)]
         pair = hidden_pair(in_order(state + [s_next]), in_order(tangent + [t_next]), w1_ref)
         yield
-        x = spread_hidden(pair[1], w2_ref[2])
-        ends = [tangent[1] + x[1], f_inner + pick(x[2], x[0]), f_middle, f_outer]
+        x = spread_hidden(pair[1], w2_side_ref[1])
+        ends = [tangent[1] + x[0], f_inner + x[1], f_middle, f_outer]
         final = jnp.concatenate(in_order(ends), axis=0)
         send(start(slot + 1) - final if slot < slots - 1 else -final, slot + 1)
 
@@ -430,16 +439,18 @@
 
     packed = width // slots % LANES == 0
     block = (slots * fields, width + width // slots) if packed else ((slots + 2) * fields, width)
-    w1, w2, w2_half, mix = pl.pallas_call(
+    w1, w2, w2_side, w2_half, w2_end, mix = pl.pallas_call(
         functools.partial(prepare_kernel, tm=tm, strips=strips, slots=slots),
         out_shape=(
             jax.ShapeDtypeStruct((WIN_OUT * channels, KEYS), BF16),
-            jax.ShapeDtypeStruct((3, 144, 2 * WIN_OUT * channels), BF16),
+            jax.ShapeDtypeStruct((144, 2 * WIN_OUT * channels), BF16),
+            jax.ShapeDtypeStruct((3, 96, 2 * WIN_OUT * channels), BF16),
             jax.ShapeDtypeStruct((96, WIN_OUT * channels), BF16),
+            jax.ShapeDtypeStruct((48, WIN_OUT * channels), BF16),
             jax.ShapeDtypeStruct((fields * time, 3 * tm * (slots + 1) * fields), BF16),
         ),
         in_specs=[VMEM] * 4,
-        out_specs=(VMEM,) * 4,
+        out_specs=(VMEM,) * 6,
         compiler_params=params(),
         name="prepare",
     )(w1_taps, bias_row, w2_taps, correlation)
@@ -447,11 +458,11 @@
     kept = pl.pallas_call(
         functools.partial(inner_kernel, strips=strips, slots=slots),
         out_shape=jax.ShapeDtypeStruct((slots, 56, cols), F32),
-        in_specs=[VMEM] * 5,
+        in_specs=[VMEM] * 7,
         out_specs=VMEM,
         compiler_params=params(),
         name="inner",
-    )(own, core_got, w1, w2, w2_half)
+    )(own, core_got, w1, w2, w2_side, w2_half, w2_end)
 
     send = pl.pallas_call(
         functools.partial(outer_kernel, strips=strips, slots=slots, parts_across=parts_across),
@@ -460,7 +471,7 @@
         out_specs=VMEM,
         compiler_params=params(),
         name="outer",
-    )(own, chip_got, kept, w1, w2)
+    )(own, chip_got, kept, w1, w2_side)
 
     blocks = lax.all_to_all(send, "tm", split_axis=0, concat_axis=0, tiled=True)
     mixed = pl.pallas_call(

time: 40.7 us -> 40.6 us (level)
  no operation moved by 1% of the time
where the time goes in v7:
time: 40.6 us; the launch traced here: 40.4 us
  blocking collectives  31 us (76%)
  Pallas kernels  8.15 us (20%)
  starting transfers between devices  1.18 us (3%)
    all_to_all x1, blocking collectives, body(): blocks = lax.all_to_all(send, 'tm', split_axis=0, concat_axis=0, tiled=True)  16.8 us
    all_to_all x1, blocking collectives, body(): back = lax.all_to_all(mixed, 'tm', split_axis=0, concat_axis=0, tiled=True)  14.2 us
    pallas_call x1, Pallas kernels, body(): pl.pallas_call(functools.partial(inner_kernel, strips=strips, slots=slots...  3.7 us
    pallas_call x1, Pallas kernels, body(): pl.pallas_call(functools.partial(outer_kernel, strips=strips, slots=slots...  1.66 us
    pallas_call x1, Pallas kernels, body(): pl.pallas_call(pack_kernel, out_shape=(whole, half, half, *loaded), in_sp...  1.25 us
    ppermute x2, starting transfers between devices, swapped(): return lax.ppermute(value, 'space', pairs + [(j, i) for i, j in pairs])  1.18 us
    pallas_call x1, Pallas kernels, body(): pl.pallas_call(place_kernel, out_shape=jax.ShapeDtypeStruct(increment.sha...  0.82 us
  transfers between devices with their start and end apart: 2, of which 0 were waited for; matrix products, arithmetic and copies ran while one was open for 0% of the time, Pallas kernels for 10%

profile of v7, /device:TPU:0, one launch (start us, length us, event | category | flops | bytes accessed | tf_op | source)
XLA Modules:
  0.0 40.4 jit_solution(2778331212468094355)
XLA Ops:
  0.0 1.2 %pack.1 = (f32[8,4,32,128]{3,2,1,0:T(8,128)S(1)}, f32[8,4,16,128]{3,2,1,0:T(8,128)S(1)}, f32[8,4,16,128]{3,2,1,0:T(8,128)S(1)}, f32[3,3,4,32]{3,2,1,0:T(4,128)S(...) custom-call(f32[4,4,8,512]{3,2,1,0:T(8,128)} %traj_hbm.1, ...), custom_call_target="tpu_custom_call" | custom-call | tf_op jit(solution)/shard_map/pack/pallas_call | solution.py:423
  1.3 0.5 %collective-permute-start.1 = (f32[8,4,16,128]{3,2,1,0:T(8,128)S(1)}, f32[8,4,16,128]{3,2,1,0:T(8,128)S(1)}, u32[]{:S(2)}, u32[]{:S(2)}) collective-permute-start(f32[8,4,16,128]{3,2,1,0:T(8,128)S(1)} %get-tuple-element.25), channel_id=1, source_target_pairs={{0,1},{2,3},{1,0},{3,2},{4,5},{6,7},{5,4},{7,6},{8,9},{10,11},{9,8... | collective-permute-start | bytes 786440 | tf_op jit(solution)/shard_map/ppermute | solution.py:435
  1.8 0.7 %collective-permute-start = (f32[8,4,16,128]{3,2,1,0:T(8,128)S(1)}, f32[8,4,16,128]{3,2,1,0:T(8,128)S(1)}, u32[]{:S(2)}, u32[]{:S(2)}) collective-permute-start(f32[8,4,16,128]{3,2,1,0:T(8,128)S(1)} %get-tuple-element.24), channel_id=1, source_target_pairs={{1,2},{2,1},{5,6},{6,5},{9,10},{10,9},{13,14},{14,13},{17,18},{18,... | collective-permute-start | bytes 786440 | tf_op jit(solution)/shard_map/ppermute | solution.py:435
  2.4 0.5 %prepare.1 = (bf16[128,256]{1,0:T(8,128)(2,1)S(1)}, bf16[144,256]{1,0:T(8,128)(2,1)S(1)}, bf16[3,96,256]{2,1,0:T(8,128)(2,1)S(1)}, bf16[96,128]{1,0:T(8,128)(2,1...) custom-call(f32[3,3,4,32]{3,2,1,0:T(4,128)S(1)} %get-tuple-element.18.w1_ref, ...), custom_call_target="tpu_custom_call" | custom-call | tf_op jit(solution)/shard_map/prepare/pallas_call | solution.py:442
  2.9 0.0 collective-permute-done.1.core_got_ref
  2.9 3.7 %inner.1.kept_ref = f32[4,56,512]{2,1,0:T(8,128)S(1)} custom-call(f32[8,4,32,128]{3,2,1,0:T(8,128)S(1)} %get-tuple-element.23.own_ref, f32[8,4,16,128]{3,2,1,0:T(8,128)S(1)} %collective-permute-done.1.core_got_ref, bf16[128,256]{1,0:T(8,128)(2,1)S(1)} %get-tuple-element.26.w1_ref, bf16[144,256]{1,0:T(8,128)(2,1)S(1)} %get-tuple-element.27.w2_ref, ...), custom_call_target="tpu_custom_call" | custom-call | tf_op jit(solution)/shard_map/inner/pallas_call | solution.py:458
  6.7 0.0 collective-permute-done.chip_got_ref
  6.7 1.7 %outer.1 = f32[8,16,640]{2,1,0:T(8,128)S(1)} custom-call(f32[8,4,32,128]{3,2,1,0:T(8,128)S(1)} %get-tuple-element.23.own_ref, f32[8,4,16,128]{3,2,1,0:T(8,128)S(1)} %collective-permute-done.chip_got_ref, f32[4,56,512]{2,1,0:T(8,128)S(1)} %inner.1.kept_ref, bf16[128,256]{1,0:T(8,128)(2,1)S(1)} %get-tuple-element.26.w1_ref, ...), custom_call_target="tpu_custom_call" | custom-call | tf_op jit(solution)/shard_map/outer/pallas_call | solution.py:467
  8.3 16.8 %all_to_all.10.block_ref = f32[8,16,640]{2,1,0:T(8,128)S(1)} all-to-all(f32[8,16,640]{2,1,0:T(8,128)S(1)} %outer.1), channel_id=1, replica_groups=mesh['tm'=8,'space'=4] {'tm'}, dimensions={0} | all-to-all | bytes 655360 | tf_op jit(solution)/shard_map/all_to_all | solution.py:476
  25.1 0.2 mix.1
  25.4 14.2 %all_to_all.11 = f32[8,4,16,128]{3,2,1,0:T(8,128)S(1)} all-to-all(f32[8,4,16,128]{3,2,1,0:T(8,128)S(1)} %mix.1), channel_id=1, replica_groups=mesh['tm'=8,'space'=4] {'tm'}, dimensions={0} | all-to-all | bytes 524288 | tf_op jit(solution)/shard_map/all_to_all | solution.py:485
  39.6 0.8 %place.1 = f32[4,4,8,512]{3,2,1,0:T(8,128)} custom-call(f32[512,128]{1,0:T(8,128)S(1)} %bitcast.4), custom_call_target="tpu_custom_call" | custom-call | tf_op jit(solution)/shard_map/place/pallas_call | solution.py:486
Async XLA Ops:
  1.3 1.7 %collective-permute-start.1 = (f32[8,4,16,128]{3,2,1,0:T(8,128)S(1)}, f32[8,4,16,128]{3,2,1,0:T(8,128)S(1)}, u32[]{:S(2)}, u32[]{:S(2)}) collective-permute-start(f32[8,4,16,128]{3,2,1,0:T(8,128)S(1)} %get-tuple-element.25), channel_id=1, source_target_pairs={{0,1},{2,3},{1,0},{3,2},{4,5},{6,7},{5,4},{7,6},{8,9},{10,11},{9,8... | collective-permute-start | bytes 786440 | tf_op jit(solution)/shard_map/ppermute | solution.py:435
  1.8 4.9 %collective-permute-start = (f32[8,4,16,128]{3,2,1,0:T(8,128)S(1)}, f32[8,4,16,128]{3,2,1,0:T(8,128)S(1)}, u32[]{:S(2)}, u32[]{:S(2)}) collective-permute-start(f32[8,4,16,128]{3,2,1,0:T(8,128)S(1)} %get-tuple-element.24), channel_id=1, source_target_pairs={{1,2},{2,1},{5,6},{6,5},{9,10},{10,9},{13,14},{14,13},{17,18},{18,... | collective-permute-start | bytes 786440 | tf_op jit(solution)/shard_map/ppermute | solution.py:435

commit v8 on v7

--- a/solution.py
+++ b/solution.py
@@ -251,10 +251,44 @@
 
 
 def inner_kernel(own_ref, core_got_ref, w1_ref, w2_ref, w2_side_ref, w2_half_ref, w2_end_ref, kept_ref, *, strips, slots):
-    even, _ = chip_side(strips)
+    even, keep = chip_side(strips)
 
     def pick(if_even, if_odd):
         return jnp.where(even, if_even, if_odd)
+
+    def in_order(values):
+        return [pick(a, b) for a, b in zip(values, values[::-1])]
+
+    def edge_slot(slot):
+        outside = jnp.zeros((8, kept_ref.shape[2]), F32)
+        lines = []
+        for index in (slot, slots + slot):
+            own = [read_group(own_ref, index, g) for g in range(4)]
+            core = [read_group(core_got_ref, index, g) for g in range(2)]
+            lines.append([outside] + in_order(own) + [pick(a, b) for a, b in zip(core, core[::-1])])
+        pairs = []
+        for start in (0, 2, 4):
+            windows = [in_order(line[start : start + 3]) for line in lines]
+            pairs.append(hidden_pair(windows[0], windows[1], w1_ref))
+            yield
+        moved_on = []
+        for kind, line in enumerate(lines):
+            a = spread_hidden(pairs[0][kind], w2_side_ref[1])
+            b = in_order(spread_hidden(pairs[1][kind], w2_ref[...]))
+            c = spread_hidden(pairs[2][kind], w2_side_ref[2])
+            added = [a[0], a[1] + b[0], b[1], b[2] + c[1], c[0]]
+            moved_on.append([outside] + [x + y for x, y in zip(line[1:6], added)])
+        s, t = moved_on
+        yield
+        near = hidden_pair(in_order(s[0:3]), in_order(t[0:3]), w1_ref)
+        middle = hidden_pair(in_order(s[2:5]), in_order(t[2:5]), w1_ref)
+        far = hidden_pair(in_order(s[4:6]), in_order(t[4:6]), w1_ref)
+        yield
+        a = spread_hidden(near[1], w2_side_ref[1])
+        b = in_order(spread_hidden(middle[1], w2_ref[...]))
+        (c,) = spread_hidden(far[1], w2_end_ref[...])
+        for g, value in enumerate([a[0], a[1] + b[0], b[1], b[2] + c]):
+            kept_ref[slot, 8 * g : 8 * g + 8, :] = t[1 + g] + value
 
     def one_slot(slot):
         line, ends = [], []
@@ -297,7 +331,13 @@
         for g, value in enumerate(kept):
             kept_ref[slot, 8 * g : 8 * g + 8, :] = value
 
-    staggered(slots, one_slot, False)
+    @pl.when(keep == 0.0)
+    def _():
+        staggered(slots, edge_slot, False)
+
+    @pl.when(keep != 0.0)
+    def _():
+        staggered(slots, one_slot, False)
 
 
 def outer_kernel(own_ref, chip_got_ref, kept_ref, w1_ref, w2_side_ref, send_ref, *, strips, slots, parts_across):
@@ -340,7 +380,7 @@
         moved_on = []
         for kind in range(2):
             w = spread_hidden(pair[kind], w2_side_ref[0])
-            moved_on.append([(frames[kind][1] + w[0]) * keep, near[kind] + w[1]])
+            moved_on.append([frames[kind][1] + w[0], near[kind] + w[1]])
         state, tangent = moved_on
         yield
         f_outer, f_middle, f_inner, s_next, t_next = [kept_ref[slot, 8 * g : 8 * g + 8, :] for g in (0, 1, 2, 5, 6)]
@@ -348,11 +388,23 @@
         yield
         x = spread_hidden(pair[1], w2_side_ref[1])
         ends = [tangent[1] + x[0], f_inner + x[1], f_middle, f_outer]
+        residual(slot, ends)
+
+    def residual(slot, ends):
         final = jnp.concatenate(in_order(ends), axis=0)
         send(start(slot + 1) - final if slot < slots - 1 else -final, slot + 1)
 
     send(start(0), 0)
-    staggered(slots, one_slot, True)
+
+    @pl.when(keep == 0.0)
+    def _():
+        for slot in range(slots):
+            residual(slot, [kept_ref[slot, 8 * g : 8 * g + 8, :] for g in range(4)])
+
+    @pl.when(keep != 0.0)
+    def _():
+        staggered(slots, one_slot, True)
+
     if not packed:
         send_ref[:, (slots + 1) * fields :, :] = jnp.zeros((rows * parts_across, fields, width), F32)
 

time: 40.6 us -> 39.6 us (0.975)
  Pallas kernels: 8.15 us -> 7.19 us
    pallas_call x1, Pallas kernels: 1.66 us -> 0.07 us  [body(): pl.pallas_call(functools.partial(outer_kernel, strips=strips, slots=slots...]
    all_to_all x1, blocking collectives: 14.2 us -> 14.9 us  [body(): back = lax.all_to_all(mixed, 'tm', split_axis=0, concat_axis=0, tiled=True)]
    all_to_all x1, blocking collectives: 16.8 us -> 16.1 us  [body(): blocks = lax.all_to_all(send, 'tm', split_axis=0, concat_axis=0, tiled=True)]
    pallas_call x1, Pallas kernels: 3.7 us -> 4.34 us  [body(): pl.pallas_call(functools.partial(inner_kernel, strips=strips, slots=slots...]
  transfers between devices with their start and end apart: 2 -> 2, of which waited for: 0 -> 0; matrix products, arithmetic and copies ran while one was open for 0% -> 0% of each run, Pallas kernels for 10% -> 12%
where the time goes in v8:
time: 39.6 us; the launch traced here: 39.4 us
  blocking collectives  31 us (78%)
  Pallas kernels  7.19 us (18%)
  starting transfers between devices  1.18 us (3%)
    all_to_all x1, blocking collectives, body(): blocks = lax.all_to_all(send, 'tm', split_axis=0, concat_axis=0, tiled=True)  16.1 us
    all_to_all x1, blocking collectives, body(): back = lax.all_to_all(mixed, 'tm', split_axis=0, concat_axis=0, tiled=True)  14.9 us
    pallas_call x1, Pallas kernels, body(): pl.pallas_call(functools.partial(inner_kernel, strips=strips, slots=slots...  4.34 us
    pallas_call x1, Pallas kernels, body(): pl.pallas_call(pack_kernel, out_shape=(whole, half, half, *loaded), in_sp...  1.25 us
    ppermute x2, starting transfers between devices, swapped(): return lax.ppermute(value, 'space', pairs + [(j, i) for i, j in pairs])  1.18 us
    pallas_call x1, Pallas kernels, body(): pl.pallas_call(place_kernel, out_shape=jax.ShapeDtypeStruct(increment.sha...  0.82 us
  transfers between devices with their start and end apart: 2, of which 0 were waited for; matrix products, arithmetic and copies ran while one was open for 0% of the time, Pallas kernels for 12%

profile of v8, /device:TPU:0, one launch (start us, length us, event | category | flops | bytes accessed | tf_op | source)
XLA Modules:
  0.0 39.4 jit_solution(7929792980949464431)
XLA Ops:
  0.0 1.2 %pack.1 = (f32[8,4,32,128]{3,2,1,0:T(8,128)S(1)}, f32[8,4,16,128]{3,2,1,0:T(8,128)S(1)}, f32[8,4,16,128]{3,2,1,0:T(8,128)S(1)}, f32[3,3,4,32]{3,2,1,0:T(4,128)S(...) custom-call(f32[4,4,8,512]{3,2,1,0:T(8,128)} %traj_hbm.1, ...), custom_call_target="tpu_custom_call" | custom-call | tf_op jit(solution)/shard_map/pack/pallas_call | solution.py:475
  1.3 0.5 %collective-permute-start.1 = (f32[8,4,16,128]{3,2,1,0:T(8,128)S(1)}, f32[8,4,16,128]{3,2,1,0:T(8,128)S(1)}, u32[]{:S(2)}, u32[]{:S(2)}) collective-permute-start(f32[8,4,16,128]{3,2,1,0:T(8,128)S(1)} %get-tuple-element.25), channel_id=1, source_target_pairs={{0,1},{2,3},{1,0},{3,2},{4,5},{6,7},{5,4},{7,6},{8,9},{10,11},{9,8... | collective-permute-start | bytes 786440 | tf_op jit(solution)/shard_map/ppermute | solution.py:487
  1.8 0.7 %collective-permute-start = (f32[8,4,16,128]{3,2,1,0:T(8,128)S(1)}, f32[8,4,16,128]{3,2,1,0:T(8,128)S(1)}, u32[]{:S(2)}, u32[]{:S(2)}) collective-permute-start(f32[8,4,16,128]{3,2,1,0:T(8,128)S(1)} %get-tuple-element.24), channel_id=1, source_target_pairs={{1,2},{2,1},{5,6},{6,5},{9,10},{10,9},{13,14},{14,13},{17,18},{18,... | collective-permute-start | bytes 786440 | tf_op jit(solution)/shard_map/ppermute | solution.py:487
  2.4 0.5 %prepare.1 = (bf16[128,256]{1,0:T(8,128)(2,1)S(1)}, bf16[144,256]{1,0:T(8,128)(2,1)S(1)}, bf16[3,96,256]{2,1,0:T(8,128)(2,1)S(1)}, bf16[96,128]{1,0:T(8,128)(2,1...) custom-call(f32[3,3,4,32]{3,2,1,0:T(4,128)S(1)} %get-tuple-element.18.w1_ref, ...), custom_call_target="tpu_custom_call" | custom-call | tf_op jit(solution)/shard_map/prepare/pallas_call | solution.py:494
  2.9 0.0 collective-permute-done.1.core_got_ref
  2.9 4.3 %inner.1.kept_ref = f32[4,56,512]{2,1,0:T(8,128)S(1)} custom-call(f32[8,4,32,128]{3,2,1,0:T(8,128)S(1)} %get-tuple-element.23.own_ref, f32[8,4,16,128]{3,2,1,0:T(8,128)S(1)} %collective-permute-done.1.core_got_ref, bf16[128,256]{1,0:T(8,128)(2,1)S(1)} %get-tuple-element.26.w1_ref, bf16[144,256]{1,0:T(8,128)(2,1)S(1)} %get-tuple-element.27.w2_ref, ...), custom_call_target="tpu_custom_call" | custom-call | tf_op jit(solution)/shard_map/inner/pallas_call | solution.py:510
  7.3 0.0 collective-permute-done.chip_got_ref
  7.3 0.1 outer.1
  7.4 16.1 %all_to_all.10.block_ref = f32[8,16,640]{2,1,0:T(8,128)S(1)} all-to-all(f32[8,16,640]{2,1,0:T(8,128)S(1)} %outer.1), channel_id=1, replica_groups=mesh['tm'=8,'space'=4] {'tm'}, dimensions={0} | all-to-all | bytes 655360 | tf_op jit(solution)/shard_map/all_to_all | solution.py:528
  23.5 0.2 mix.1
  23.7 14.9 %all_to_all.11 = f32[8,4,16,128]{3,2,1,0:T(8,128)S(1)} all-to-all(f32[8,4,16,128]{3,2,1,0:T(8,128)S(1)} %mix.1), channel_id=1, replica_groups=mesh['tm'=8,'space'=4] {'tm'}, dimensions={0} | all-to-all | bytes 524288 | tf_op jit(solution)/shard_map/all_to_all | solution.py:537
  38.6 0.8 %place.1 = f32[4,4,8,512]{3,2,1,0:T(8,128)} custom-call(f32[512,128]{1,0:T(8,128)S(1)} %bitcast.4), custom_call_target="tpu_custom_call" | custom-call | tf_op jit(solution)/shard_map/place/pallas_call | solution.py:538
Async XLA Ops:
  1.3 1.7 %collective-permute-start.1 = (f32[8,4,16,128]{3,2,1,0:T(8,128)S(1)}, f32[8,4,16,128]{3,2,1,0:T(8,128)S(1)}, u32[]{:S(2)}, u32[]{:S(2)}) collective-permute-start(f32[8,4,16,128]{3,2,1,0:T(8,128)S(1)} %get-tuple-element.25), channel_id=1, source_target_pairs={{0,1},{2,3},{1,0},{3,2},{4,5},{6,7},{5,4},{7,6},{8,9},{10,11},{9,8... | collective-permute-start | bytes 786440 | tf_op jit(solution)/shard_map/ppermute | solution.py:487
  1.8 5.5 %collective-permute-start = (f32[8,4,16,128]{3,2,1,0:T(8,128)S(1)}, f32[8,4,16,128]{3,2,1,0:T(8,128)S(1)}, u32[]{:S(2)}, u32[]{:S(2)}) collective-permute-start(f32[8,4,16,128]{3,2,1,0:T(8,128)S(1)} %get-tuple-element.24), channel_id=1, source_target_pairs={{1,2},{2,1},{5,6},{6,5},{9,10},{10,9},{13,14},{14,13},{17,18},{18,... | collective-permute-start | bytes 786440 | tf_op jit(solution)/shard_map/ppermute | solution.py:487

commit v9 on v8

--- a/solution.py
+++ b/solution.py
@@ -240,8 +240,8 @@
     return jnp.concatenate([ref[index, p, 8 * g : 8 * g + 8, :] for p in range(pieces)], axis=1)
 
 
-def staggered(slots, one_slot, together):
-    waiting = [one_slot(slot) for slot in range(slots)]
+def staggered(slots, one_slot, together, first=0):
+    waiting = [one_slot(first + slot) for slot in range(slots)]
     running = []
     while waiting or running:
         starting = len(waiting) if together else 1
@@ -340,7 +340,7 @@
         staggered(slots, one_slot, False)
 
 
-def outer_kernel(own_ref, chip_got_ref, kept_ref, w1_ref, w2_side_ref, send_ref, *, strips, slots, parts_across):
+def outer_kernel(own_ref, chip_got_ref, kept_ref, w1_ref, w2_side_ref, send_ref, done_ref, *, strips, slots, parts_across):
     even, keep = chip_side(strips)
     cols = kept_ref.shape[2]
     width = cols // parts_across
@@ -388,10 +388,11 @@
         yield
         x = spread_hidden(pair[1], w2_side_ref[1])
         ends = [tangent[1] + x[0], f_inner + x[1], f_middle, f_outer]
-        residual(slot, ends)
-
-    def residual(slot, ends):
-        final = jnp.concatenate(in_order(ends), axis=0)
+        for g, value in enumerate(ends):
+            done_ref[slot, 8 * g : 8 * g + 8, :] = value
+
+    def residual(slot, ref):
+        final = jnp.concatenate(in_order([ref[slot, 8 * g : 8 * g + 8, :] for g in range(4)]), axis=0)
         send(start(slot + 1) - final if slot < slots - 1 else -final, slot + 1)
 
     send(start(0), 0)
@@ -399,11 +400,17 @@
     @pl.when(keep == 0.0)
     def _():
         for slot in range(slots):
-            residual(slot, [kept_ref[slot, 8 * g : 8 * g + 8, :] for g in range(4)])
+            residual(slot, kept_ref)
 
     @pl.when(keep != 0.0)
     def _():
-        staggered(slots, one_slot, True)
+        def some_slots(turn, carry):
+            staggered(2, one_slot, True, 2 * turn)
+            return carry
+
+        lax.fori_loop(0, slots // 2, some_slots, 0)
+        for slot in range(slots):
+            residual(slot, done_ref)
 
     if not packed:
         send_ref[:, (slots + 1) * fields :, :] = jnp.zeros((rows * parts_across, fields, width), F32)
@@ -521,6 +528,7 @@
         out_shape=jax.ShapeDtypeStruct((tm, *block), F32),
         in_specs=[VMEM] * 5,
         out_specs=VMEM,
+        scratch_shapes=[pltpu.VMEM((slots, rows * fields, cols), F32)],
         compiler_params=params(),
         name="outer",
     )(own, chip_got, kept, w1, w2_side)

time: 39.6 us -> 38.4 us (0.970)
  the two profiles are of different devices: /device:TPU:0 before, /device:TPU:4 now
where the time goes in v9:
time: 38.4 us; the launch traced here: 38.2 us
  blocking collectives  25.4 us (66%)
  Pallas kernels  9.06 us (24%)
  starting transfers between devices  1.99 us (5%)
  waiting for transfers between devices  1.61 us (4%)
    all_to_all x1, blocking collectives, body(): blocks = lax.all_to_all(send, 'tm', split_axis=0, concat_axis=0, tiled=True)  14.7 us
    all_to_all x1, blocking collectives, body(): back = lax.all_to_all(mixed, 'tm', split_axis=0, concat_axis=0, tiled=True)  10.7 us
    pallas_call x1, Pallas kernels, body(): pl.pallas_call(functools.partial(inner_kernel, strips=strips, slots=slots...  3.65 us
    pallas_call x1, Pallas kernels, body(): pl.pallas_call(functools.partial(outer_kernel, strips=strips, slots=slots...  2.63 us
    ppermute x2, starting transfers between devices, swapped(): return lax.ppermute(value, 'space', pairs + [(j, i) for i, j in pairs])  1.99 us
    ppermute x2, waiting for transfers between devices, swapped(): return lax.ppermute(value, 'space', pairs + [(j, i) for i, j in pairs])  1.61 us
    pallas_call x1, Pallas kernels, body(): pl.pallas_call(pack_kernel, out_shape=(whole, half, half, *loaded), in_sp...  1.25 us
    pallas_call x1, Pallas kernels, body(): pl.pallas_call(place_kernel, out_shape=jax.ShapeDtypeStruct(increment.sha...  0.82 us
  transfers between devices with their start and end apart: 2, of which 1 were waited for; matrix products, arithmetic and copies ran while one was open for 0% of the time, Pallas kernels for 11%

profile of v9, /device:TPU:4, one launch (start us, length us, event | category | flops | bytes accessed | tf_op | source)
XLA Modules:
  0.0 38.2 jit_solution(16790807109995050622)
XLA Ops:
  0.0 1.2 %pack.1 = (f32[8,4,32,128]{3,2,1,0:T(8,128)S(1)}, f32[8,4,16,128]{3,2,1,0:T(8,128)S(1)}, f32[8,4,16,128]{3,2,1,0:T(8,128)S(1)}, f32[3,3,4,32]{3,2,1,0:T(4,128)S(...) custom-call(f32[4,4,8,512]{3,2,1,0:T(8,128)} %traj_hbm.1, ...), custom_call_target="tpu_custom_call" | custom-call | tf_op jit(solution)/shard_map/pack/pallas_call | solution.py:482
  1.3 0.1 collective-permute-start.1
  1.3 1.9 %collective-permute-start = (f32[8,4,16,128]{3,2,1,0:T(8,128)S(1)}, f32[8,4,16,128]{3,2,1,0:T(8,128)S(1)}, u32[]{:S(2)}, u32[]{:S(2)}) collective-permute-start(f32[8,4,16,128]{3,2,1,0:T(8,128)S(1)} %get-tuple-element.24), channel_id=1, source_target_pairs={{1,2},{2,1},{5,6},{6,5},{9,10},{10,9},{13,14},{14,13},{17,18},{18,... | collective-permute-start | bytes 786440 | tf_op jit(solution)/shard_map/ppermute | solution.py:494
  3.3 0.5 %prepare.1 = (bf16[128,256]{1,0:T(8,128)(2,1)S(1)}, bf16[144,256]{1,0:T(8,128)(2,1)S(1)}, bf16[3,96,256]{2,1,0:T(8,128)(2,1)S(1)}, bf16[96,128]{1,0:T(8,128)(2,1...) custom-call(f32[3,3,4,32]{3,2,1,0:T(4,128)S(1)} %get-tuple-element.18.w1_ref, ...), custom_call_target="tpu_custom_call" | custom-call | tf_op jit(solution)/shard_map/prepare/pallas_call | solution.py:501
  3.7 0.0 collective-permute-done.1.core_got_ref
  3.8 3.7 %inner.1.kept_ref = f32[4,56,512]{2,1,0:T(8,128)S(1)} custom-call(f32[8,4,32,128]{3,2,1,0:T(8,128)S(1)} %get-tuple-element.23.own_ref, f32[8,4,16,128]{3,2,1,0:T(8,128)S(1)} %collective-permute-done.1.core_got_ref, bf16[128,256]{1,0:T(8,128)(2,1)S(1)} %get-tuple-element.26.w1_ref, bf16[144,256]{1,0:T(8,128)(2,1)S(1)} %get-tuple-element.27.w2_ref, ...), custom_call_target="tpu_custom_call" | custom-call | tf_op jit(solution)/shard_map/inner/pallas_call | solution.py:517
  7.4 1.6 %collective-permute-done.chip_got_ref = f32[8,4,16,128]{3,2,1,0:T(8,128)S(1)} collective-permute-done((f32[8,4,16,128]{3,2,1,0:T(8,128)S(1)}, f32[8,4,16,128]{3,2,1,0:T(8,128)S(1)}, u32[]{:S(2)}, u32[]{:S(2)}) %collective-permute-start) | collective-permute-done | bytes 262176 | tf_op jit(solution)/shard_map/ppermute | solution.py:494
  9.0 2.6 %outer.1 = f32[8,16,640]{2,1,0:T(8,128)S(1)} custom-call(f32[8,4,32,128]{3,2,1,0:T(8,128)S(1)} %get-tuple-element.23.own_ref, f32[8,4,16,128]{3,2,1,0:T(8,128)S(1)} %collective-permute-done.chip_got_ref, f32[4,56,512]{2,1,0:T(8,128)S(1)} %inner.1.kept_ref, bf16[128,256]{1,0:T(8,128)(2,1)S(1)} %get-tuple-element.26.w1_ref, ...), custom_call_target="tpu_custom_call" | custom-call | tf_op jit(solution)/shard_map/outer/pallas_call | solution.py:526
  11.7 14.7 %all_to_all.10.block_ref = f32[8,16,640]{2,1,0:T(8,128)S(1)} all-to-all(f32[8,16,640]{2,1,0:T(8,128)S(1)} %outer.1), channel_id=1, replica_groups=mesh['tm'=8,'space'=4] {'tm'}, dimensions={0} | all-to-all | bytes 655360 | tf_op jit(solution)/shard_map/all_to_all | solution.py:536
  26.4 0.2 mix.1
  26.6 10.7 %all_to_all.11 = f32[8,4,16,128]{3,2,1,0:T(8,128)S(1)} all-to-all(f32[8,4,16,128]{3,2,1,0:T(8,128)S(1)} %mix.1), channel_id=1, replica_groups=mesh['tm'=8,'space'=4] {'tm'}, dimensions={0} | all-to-all | bytes 524288 | tf_op jit(solution)/shard_map/all_to_all | solution.py:545
  37.4 0.8 %place.1 = f32[4,4,8,512]{3,2,1,0:T(8,128)} custom-call(f32[512,128]{1,0:T(8,128)S(1)} %bitcast.4), custom_call_target="tpu_custom_call" | custom-call | tf_op jit(solution)/shard_map/place/pallas_call | solution.py:546
Async XLA Ops:
  1.3 2.5 %collective-permute-start.1 = (f32[8,4,16,128]{3,2,1,0:T(8,128)S(1)}, f32[8,4,16,128]{3,2,1,0:T(8,128)S(1)}, u32[]{:S(2)}, u32[]{:S(2)}) collective-permute-start(f32[8,4,16,128]{3,2,1,0:T(8,128)S(1)} %get-tuple-element.25), channel_id=1, source_target_pairs={{0,1},{2,3},{1,0},{3,2},{4,5},{6,7},{5,4},{7,6},{8,9},{10,11},{9,8... | collective-permute-start | bytes 786440 | tf_op jit(solution)/shard_map/ppermute | solution.py:494
  1.3 7.7 %collective-permute-start = (f32[8,4,16,128]{3,2,1,0:T(8,128)S(1)}, f32[8,4,16,128]{3,2,1,0:T(8,128)S(1)}, u32[]{:S(2)}, u32[]{:S(2)}) collective-permute-start(f32[8,4,16,128]{3,2,1,0:T(8,128)S(1)} %get-tuple-element.24), channel_id=1, source_target_pairs={{1,2},{2,1},{5,6},{6,5},{9,10},{10,9},{13,14},{14,13},{17,18},{18,... | collective-permute-start | bytes 786440 | tf_op jit(solution)/shard_map/ppermute | solution.py:494

commit v10 on v9

--- a/solution.py
+++ b/solution.py
@@ -402,13 +402,20 @@
         for slot in range(slots):
             residual(slot, kept_ref)
 
-    @pl.when(keep != 0.0)
+    @pl.when((keep != 0.0) & even)
+    def _():
+        staggered(slots, one_slot, True)
+
+    @pl.when((keep != 0.0) & ~even)
     def _():
         def some_slots(turn, carry):
             staggered(2, one_slot, True, 2 * turn)
             return carry
 
         lax.fori_loop(0, slots // 2, some_slots, 0)
+
+    @pl.when(keep != 0.0)
+    def _():
         for slot in range(slots):
             residual(slot, done_ref)
 

time: 38.4 us -> 37.5 us (0.977)
  Pallas kernels: 9.06 us -> 8.15 us
    pallas_call x1, Pallas kernels: 2.63 us -> 1.71 us  [body(): pl.pallas_call(functools.partial(outer_kernel, strips=strips, slots=slots...]
where the time goes in v10:
time: 37.5 us; the launch traced here: 37.3 us
  blocking collectives  25.4 us (68%)
  Pallas kernels  8.15 us (22%)
  starting transfers between devices  1.99 us (5%)
  waiting for transfers between devices  1.61 us (4%)
    all_to_all x1, blocking collectives, body(): blocks = lax.all_to_all(send, 'tm', split_axis=0, concat_axis=0, tiled=True)  14.6 us
    all_to_all x1, blocking collectives, body(): back = lax.all_to_all(mixed, 'tm', split_axis=0, concat_axis=0, tiled=True)  10.8 us
    pallas_call x1, Pallas kernels, body(): pl.pallas_call(functools.partial(inner_kernel, strips=strips, slots=slots...  3.65 us
    ppermute x2, starting transfers between devices, swapped(): return lax.ppermute(value, 'space', pairs + [(j, i) for i, j in pairs])  1.99 us
    pallas_call x1, Pallas kernels, body(): pl.pallas_call(functools.partial(outer_kernel, strips=strips, slots=slots...  1.71 us
    ppermute x2, waiting for transfers between devices, swapped(): return lax.ppermute(value, 'space', pairs + [(j, i) for i, j in pairs])  1.61 us
    pallas_call x1, Pallas kernels, body(): pl.pallas_call(pack_kernel, out_shape=(whole, half, half, *loaded), in_sp...  1.25 us
    pallas_call x1, Pallas kernels, body(): pl.pallas_call(place_kernel, out_shape=jax.ShapeDtypeStruct(increment.sha...  0.82 us
  transfers between devices with their start and end apart: 2, of which 1 were waited for; matrix products, arithmetic and copies ran while one was open for 0% of the time, Pallas kernels for 11%

profile of v10, /device:TPU:4, one launch (start us, length us, event | category | flops | bytes accessed | tf_op | source)
XLA Modules:
  0.0 37.3 jit_solution(14936653978141910640)
XLA Ops:
  0.0 1.2 %pack.1 = (f32[8,4,32,128]{3,2,1,0:T(8,128)S(1)}, f32[8,4,16,128]{3,2,1,0:T(8,128)S(1)}, f32[8,4,16,128]{3,2,1,0:T(8,128)S(1)}, f32[3,3,4,32]{3,2,1,0:T(4,128)S(...) custom-call(f32[4,4,8,512]{3,2,1,0:T(8,128)} %traj_hbm.1, ...), custom_call_target="tpu_custom_call" | custom-call | tf_op jit(solution)/shard_map/pack/pallas_call | solution.py:489
  1.3 0.1 collective-permute-start.1
  1.3 1.9 %collective-permute-start = (f32[8,4,16,128]{3,2,1,0:T(8,128)S(1)}, f32[8,4,16,128]{3,2,1,0:T(8,128)S(1)}, u32[]{:S(2)}, u32[]{:S(2)}) collective-permute-start(f32[8,4,16,128]{3,2,1,0:T(8,128)S(1)} %get-tuple-element.24), channel_id=1, source_target_pairs={{1,2},{2,1},{5,6},{6,5},{9,10},{10,9},{13,14},{14,13},{17,18},{18,... | collective-permute-start | bytes 786440 | tf_op jit(solution)/shard_map/ppermute | solution.py:501
  3.3 0.5 %prepare.1 = (bf16[128,256]{1,0:T(8,128)(2,1)S(1)}, bf16[144,256]{1,0:T(8,128)(2,1)S(1)}, bf16[3,96,256]{2,1,0:T(8,128)(2,1)S(1)}, bf16[96,128]{1,0:T(8,128)(2,1...) custom-call(f32[3,3,4,32]{3,2,1,0:T(4,128)S(1)} %get-tuple-element.18.w1_ref, ...), custom_call_target="tpu_custom_call" | custom-call | tf_op jit(solution)/shard_map/prepare/pallas_call | solution.py:508
  3.7 0.0 collective-permute-done.1.core_got_ref
  3.8 3.7 %inner.1.kept_ref = f32[4,56,512]{2,1,0:T(8,128)S(1)} custom-call(f32[8,4,32,128]{3,2,1,0:T(8,128)S(1)} %get-tuple-element.23.own_ref, f32[8,4,16,128]{3,2,1,0:T(8,128)S(1)} %collective-permute-done.1.core_got_ref, bf16[128,256]{1,0:T(8,128)(2,1)S(1)} %get-tuple-element.26.w1_ref, bf16[144,256]{1,0:T(8,128)(2,1)S(1)} %get-tuple-element.27.w2_ref, ...), custom_call_target="tpu_custom_call" | custom-call | tf_op jit(solution)/shard_map/inner/pallas_call | solution.py:524
  7.4 1.6 %collective-permute-done.chip_got_ref = f32[8,4,16,128]{3,2,1,0:T(8,128)S(1)} collective-permute-done((f32[8,4,16,128]{3,2,1,0:T(8,128)S(1)}, f32[8,4,16,128]{3,2,1,0:T(8,128)S(1)}, u32[]{:S(2)}, u32[]{:S(2)}) %collective-permute-start) | collective-permute-done | bytes 262176 | tf_op jit(solution)/shard_map/ppermute | solution.py:501
  9.0 1.7 %outer.1 = f32[8,16,640]{2,1,0:T(8,128)S(1)} custom-call(f32[8,4,32,128]{3,2,1,0:T(8,128)S(1)} %get-tuple-element.23.own_ref, f32[8,4,16,128]{3,2,1,0:T(8,128)S(1)} %collective-permute-done.chip_got_ref, f32[4,56,512]{2,1,0:T(8,128)S(1)} %inner.1.kept_ref, bf16[128,256]{1,0:T(8,128)(2,1)S(1)} %get-tuple-element.26.w1_ref, ...), custom_call_target="tpu_custom_call" | custom-call | tf_op jit(solution)/shard_map/outer/pallas_call | solution.py:533
  10.8 14.6 %all_to_all.10.block_ref = f32[8,16,640]{2,1,0:T(8,128)S(1)} all-to-all(f32[8,16,640]{2,1,0:T(8,128)S(1)} %outer.1), channel_id=1, replica_groups=mesh['tm'=8,'space'=4] {'tm'}, dimensions={0} | all-to-all | bytes 655360 | tf_op jit(solution)/shard_map/all_to_all | solution.py:543
  25.4 0.2 mix.1
  25.6 10.8 %all_to_all.11 = f32[8,4,16,128]{3,2,1,0:T(8,128)S(1)} all-to-all(f32[8,4,16,128]{3,2,1,0:T(8,128)S(1)} %mix.1), channel_id=1, replica_groups=mesh['tm'=8,'space'=4] {'tm'}, dimensions={0} | all-to-all | bytes 524288 | tf_op jit(solution)/shard_map/all_to_all | solution.py:552
  36.4 0.8 %place.1 = f32[4,4,8,512]{3,2,1,0:T(8,128)} custom-call(f32[512,128]{1,0:T(8,128)S(1)} %bitcast.4), custom_call_target="tpu_custom_call" | custom-call | tf_op jit(solution)/shard_map/place/pallas_call | solution.py:553
Async XLA Ops:
  1.3 2.5 %collective-permute-start.1 = (f32[8,4,16,128]{3,2,1,0:T(8,128)S(1)}, f32[8,4,16,128]{3,2,1,0:T(8,128)S(1)}, u32[]{:S(2)}, u32[]{:S(2)}) collective-permute-start(f32[8,4,16,128]{3,2,1,0:T(8,128)S(1)} %get-tuple-element.25), channel_id=1, source_target_pairs={{0,1},{2,3},{1,0},{3,2},{4,5},{6,7},{5,4},{7,6},{8,9},{10,11},{9,8... | collective-permute-start | bytes 786440 | tf_op jit(solution)/shard_map/ppermute | solution.py:501
  1.3 7.7 %collective-permute-start = (f32[8,4,16,128]{3,2,1,0:T(8,128)S(1)}, f32[8,4,16,128]{3,2,1,0:T(8,128)S(1)}, u32[]{:S(2)}, u32[]{:S(2)}) collective-permute-start(f32[8,4,16,128]{3,2,1,0:T(8,128)S(1)} %get-tuple-element.24), channel_id=1, source_target_pairs={{1,2},{2,1},{5,6},{6,5},{9,10},{10,9},{13,14},{14,13},{17,18},{18,... | collective-permute-start | bytes 786440 | tf_op jit(solution)/shard_map/ppermute | solution.py:501
